TPU v7x, 32 devices: a whole 2x2x4 slice. The times are simulated.
32 devices in a mesh: dp: 4 (over y, x), fsdp: 8 (over z, core).
Axes of the slice: x: 2, y: 2, z: 4, core: 2. Of those that a mesh axis runs over, the one named last changes fastest.
Arguments:
- block_input: bfloat16 [4, 2, 2048, 1536], P('dp', None, 'fsdp'), may hold values from -6 to 6
- seq_lengths: int32 [4, 2, 3], P('dp'), may hold values from 0 to 2048, as said below
- adapter_ids: int32 [4, 2, 3], P('dp'), may hold values from 0 to 7
- norm_gain: float32 [1536], replicated, may hold values from 0.5 to 1.5
- w_in: bfloat16 [1536, 6400], P('fsdp'), may hold values from -0.15625 to 0.15625
- w_dt: bfloat16 [1536, 48], P('fsdp'), may hold values from -0.15625 to 0.15625
- conv_weight: float32 [4, 3328], replicated, may hold values from -3 to 3
- conv_bias: float32 [3328], replicated, may hold values from -0.5 to 0.5
- dt_bias: float32 [48], replicated, may hold values from -3 to -1
- head_rates: float32 [48], replicated, may hold values from 0.00048828125 to 0.3
- skip_gain: float32 [48], replicated, may hold values from 0.5 to 1.5
- gate_gain: float32 [3072], replicated, may hold values from 0.5 to 1.5
- w_out: bfloat16 [3072, 1536], P('fsdp'), may hold values from -0.109375 to 0.109375
- in_down: bfloat16 [8, 16, 1536], replicated, may hold values from -0.15625 to 0.15625
- in_up: bfloat16 [8, 16, 6400], replicated, may hold values from -1.5 to 1.5
- out_down: bfloat16 [8, 16, 3072], replicated, may hold values from -0.109375 to 0.109375
- out_up: bfloat16 [8, 16, 1536], replicated, may hold values from -1.5 to 1.5
- out_grad: bfloat16 [4, 2, 2048, 1536], P('dp', None, 'fsdp'), may hold values from -6 to 6
Outputs:
- block_output: bfloat16 [4, 2, 2048, 1536], P('dp', None, 'fsdp')
- input_grad: float32 [4, 2, 2048, 1536], P('dp', None, 'fsdp')
- grad_in_down: float32 [8, 16, 1536], P(None, None, 'fsdp')
- grad_in_up: float32 [8, 16, 6400], P(None, None, 'fsdp')
- grad_out_down: float32 [8, 16, 3072], P(None, None, 'fsdp')
- grad_out_up: float32 [8, 16, 1536], P(None, None, 'fsdp')
Inputs may be any that keep to these rules, and one draw needn't show every extreme that they name: `seq_lengths`: in every stream the lengths sum to at most 2048, the rest of the stream being padding; each length is 0 or at least 1024; in every group one stream holds a single sequence of 2048 positions.
All inputs are finite; a program needn't handle non-finite values.
Results may differ from a plain program's by a relative error of at most 0.0074.
Values may be sent and summed in bfloat16 or wider, within the bound.
No kernel may reach another device: no remote copies, remote signals or barrier semaphores. Data moves between devices by JAX's collectives and lax.ppermute only.
A program may use at most 384 MiB of HBM per device.

v0:
```python
import jax
import jax.numpy as jnp
from jax import lax
from jax.sharding import PartitionSpec as P

EPSILON = 1e-05
HIGHEST = lax.Precision.HIGHEST


def shifted(block, axis, distance):
    devices = range(lax.axis_size(axis))
    route = [(i - distance, i) for i in devices if i - distance in devices]
    return lax.ppermute(block, axis, route)


def prefix(part, axis, combine, identity, reverse):
    count = lax.axis_size(axis)
    place = lax.axis_index(axis)
    ahead = count - 1 - place if reverse else place
    gathered = jax.tree.map(lambda a: lax.all_gather(a, axis), part)
    state = jax.tree.map(lambda a, e: jnp.zeros_like(a) + jnp.asarray(e, a.dtype), part, identity)

    def one(hop, state):
        source = count - 1 - hop if reverse else hop
        return combine(
            state, jax.tree.map(lambda a: lax.dynamic_index_in_dim(a, source, 0, False), gathered)
        )

    return lax.fori_loop(0, ahead, one, state)


def rms_scale(values, gain_vec):
    mean_sq = jnp.mean(values * values, axis=-1, keepdims=True)
    return values * lax.rsqrt(mean_sq + EPSILON) * gain_vec


def segment_ids(seq_lens, positions):
    seg_ends = jnp.cumsum(seq_lens, axis=-1, dtype=jnp.int32)
    counted = jnp.sum(
        (positions[None, :, None] >= seg_ends[:, None, :]).astype(jnp.int32),
        axis=-1,
        dtype=jnp.int32,
    )
    return jnp.where(positions[None, :] < 0, -1, counted)


def tap_masks(seg_ext, conv_taps, length):
    own_seg = seg_ext[:, conv_taps - 1 :]
    return jnp.stack(
        [
            (seg_ext[:, offset : offset + length] == own_seg).astype(jnp.float32)
            for offset in range(conv_taps)
        ],
        axis=-1,
    )


def adapter_table(segment, seq_ids, adapters):
    kinds = jnp.arange(adapters, dtype=jnp.int32)
    chosen = (seq_ids[:, :, None] == kinds[None, None, :]).astype(jnp.float32)
    slot_range = jnp.arange(seq_ids.shape[1], dtype=jnp.int32)
    member = (segment[:, :, None] == slot_range[None, None, :]).astype(jnp.float32)
    return jnp.einsum("slj,sjk->slk", member, chosen, precision=HIGHEST)


def convolve(extended, tap_valid, conv_weight, conv_bias):
    length = tap_valid.shape[1]
    running = conv_bias
    for offset in range(conv_weight.shape[0]):
        running = (
            running
            + conv_weight[offset]
            * extended[:, offset : offset + length, :]
            * tap_valid[:, :, offset, None]
        )
    return jax.nn.silu(running)


def span_masks(segment, prior_seg):
    length = segment.shape[1]
    in_span = jnp.arange(length, dtype=jnp.int32)
    pair_mask = (in_span[None, :, None] >= in_span[None, None, :]) & (
        segment[:, :, None] == segment[:, None, :]
    )
    enter_mask = (segment == prior_seg[:, None]).astype(jnp.float32)
    last_seg = segment[:, -1]
    last_mask = (segment == last_seg[:, None]).astype(jnp.float32)
    carry_mask = (last_seg == prior_seg).astype(jnp.float32)
    return (pair_mask, enter_mask, last_mask, carry_mask)


def span_summary(conv_x, step_size, input_b, head_rates, last_mask, carry_mask):
    streams, length, inner = conv_x.shape
    heads = head_rates.shape[0]
    log_decay = jnp.cumsum(-step_size * head_rates, axis=1)
    weight = jnp.exp(log_decay[:, -1:, :] - log_decay) * step_size * last_mask[:, :, None]
    heads_x = conv_x.reshape(streams, length, heads, inner // heads)
    span_state = jnp.einsum("slhp,sln,slh->shpn", heads_x, input_b, weight, precision=HIGHEST)
    through = carry_mask[:, None] * jnp.exp(log_decay[:, -1, :])
    return (through, span_state)


def span_mix(
    conv_x, step_size, input_b, output_c, state_in, head_rates, skip_gain, pair_mask, enter_mask
):
    streams, length, inner = conv_x.shape
    heads = head_rates.shape[0]
    log_decay = jnp.cumsum(-step_size * head_rates, axis=1)
    by_head = jnp.transpose(log_decay, (0, 2, 1))
    decay_gap = by_head[:, :, :, None] - by_head[:, :, None, :]
    decay_mat = jnp.exp(jnp.where(pair_mask[:, None, :, :], decay_gap, -1e30))
    c_dot_b = jnp.einsum("sln,smn->slm", output_c, input_b, precision=HIGHEST)
    heads_x = conv_x.reshape(streams, length, heads, inner // heads)
    scaled_x = heads_x * step_size[:, :, :, None]
    inside = jnp.einsum("slm,shlm,smhp->slhp", c_dot_b, decay_mat, scaled_x, precision=HIGHEST)
    entering = enter_mask[:, :, None] * jnp.exp(log_decay)
    outside = (
        jnp.einsum("sln,shpn->slhp", output_c, state_in, precision=HIGHEST)
        * entering[:, :, :, None]
    )
    mixed_out = inside + outside + skip_gain[:, None] * heads_x
    return mixed_out.reshape(streams, length, inner)


def pass_state(earlier, later_part):
    return (
        earlier[0] * later_part[0],
        later_part[0][:, :, None, None] * earlier[1] + later_part[1],
    )


def local(
    block_input,
    seq_lengths,
    adapter_ids,
    norm_gain,
    w_in,
    w_dt,
    conv_weight,
    conv_bias,
    dt_bias,
    head_rates,
    skip_gain,
    gate_gain,
    w_out,
    in_down,
    in_up,
    out_down,
    out_up,
    out_grad,
):
    streams, length, width = (block_input.shape[1], block_input.shape[2], block_input.shape[3])
    inner = gate_gain.shape[0]
    conv_taps, conv_cols = conv_weight.shape
    heads = dt_bias.shape[0]
    state_size = (conv_cols - inner) // 2
    adapters, ranks = (in_down.shape[0], in_down.shape[1])
    in_cols = in_up.shape[2]
    slots = seq_lengths.shape[2]
    row_count = streams * length
    first_pos = lax.axis_index("fsdp") * length
    positions = first_pos - (conv_taps - 1) + jnp.arange(length + conv_taps - 1, dtype=jnp.int32)
    seg_ext = segment_ids(seq_lengths[0], positions)
    segment = seg_ext[:, conv_taps - 1 :]
    prior_seg = seg_ext[:, conv_taps - 2]
    tap_valid = tap_masks(seg_ext, conv_taps, length)
    pair_mask, enter_mask, last_mask, carry_mask = span_masks(segment, prior_seg)
    valid_rows = (segment < slots).astype(jnp.float32).reshape(row_count, 1)
    onehot = adapter_table(segment, adapter_ids[0], adapters).reshape(row_count, adapters)
    inputs = block_input.reshape(row_count, width).astype(jnp.float32)

    def norm_part(values):
        return rms_scale(values, norm_gain)

    normed, norm_pull = jax.vjp(norm_part, inputs)
    normed_low = normed.astype(jnp.bfloat16)
    pieces = (
        lax.all_gather(w_in, "fsdp", axis=0, tiled=True),
        lax.all_gather(w_dt, "fsdp", axis=0, tiled=True),
    )
    columns = normed_low
    projected = jnp.dot(columns, pieces[0], preferred_element_type=jnp.float32)
    dt_raw = jnp.dot(columns, pieces[1], preferred_element_type=jnp.float32)
    hidden_in = (
        jnp.einsum("rd,kqd->rkq", normed_low, in_down, preferred_element_type=jnp.float32)
        * onehot[:, :, None]
    ).astype(jnp.bfloat16)
    projected = projected + jnp.dot(
        hidden_in.reshape(row_count, adapters * ranks),
        in_up.reshape(adapters * ranks, in_cols),
        preferred_element_type=jnp.float32,
    )
    proj_low = projected.astype(jnp.bfloat16)
    gate_in = proj_low[:, :inner].astype(jnp.float32)
    conv_in = proj_low[:, inner:].reshape(streams, length, conv_cols)
    prior_rows = shifted(conv_in[:, length - conv_taps + 1 :, :], "fsdp", 1)
    extended = jnp.concatenate([prior_rows, conv_in], axis=1).astype(jnp.float32)

    def conv_part(values):
        return convolve(values, tap_valid, conv_weight, conv_bias)

    conv_out, conv_pull = jax.vjp(conv_part, extended)
    conv_x = conv_out[:, :, :inner]
    input_b = conv_out[:, :, inner : inner + state_size]
    output_c = conv_out[:, :, inner + state_size :]

    def step_part(values):
        return jax.nn.softplus(values + dt_bias)

    step_size, step_pull = jax.vjp(step_part, dt_raw.reshape(streams, length, heads))

    def summary_part(values_x, values_step, values_b):
        return span_summary(values_x, values_step, values_b, head_rates, last_mask, carry_mask)

    (through, span_state), summary_pull = jax.vjp(summary_part, conv_x, step_size, input_b)
    carried = prefix(
        (through, span_state),
        "fsdp",
        pass_state,
        (jnp.ones_like(through), jnp.zeros_like(span_state)),
        False,
    )
    state_in = carried[1]

    def mix_part(values_x, values_step, values_b, values_c, values_state):
        return span_mix(
            values_x,
            values_step,
            values_b,
            values_c,
            values_state,
            head_rates,
            skip_gain,
            pair_mask,
            enter_mask,
        )

    mixed_out, mix_pull = jax.vjp(mix_part, conv_x, step_size, input_b, output_c, state_in)

    def gate_part(values, gate_values):
        return rms_scale(values * jax.nn.silu(gate_values), gate_gain)

    normed_out, gate_pull = jax.vjp(gate_part, mixed_out.reshape(row_count, inner), gate_in)
    out_low = normed_out.astype(jnp.bfloat16)
    columns = out_low
    branch = jnp.dot(
        columns,
        lax.all_gather(w_out, "fsdp", axis=0, tiled=True),
        preferred_element_type=jnp.float32,
    )
    hidden_out = (
        jnp.einsum("ri,kqi->rkq", out_low, out_down, preferred_element_type=jnp.float32)
        * onehot[:, :, None]
    ).astype(jnp.bfloat16)
    branch = branch + jnp.dot(
        hidden_out.reshape(row_count, adapters * ranks),
        out_up.reshape(adapters * ranks, width),
        preferred_element_type=jnp.float32,
    )
    branch = branch * valid_rows
    block_output = (inputs + branch).astype(jnp.bfloat16).reshape(1, streams, length, width)
    grad_rows = out_grad.reshape(row_count, width).astype(jnp.float32)
    d_branch = (grad_rows * valid_rows).astype(jnp.bfloat16)
    d_hidden_out = (
        jnp.einsum("rd,kqd->rkq", d_branch, out_up, preferred_element_type=jnp.float32)
        * onehot[:, :, None]
    ).astype(jnp.bfloat16)
    d_normed_out = jnp.einsum(
        "rd,id->ri",
        d_branch,
        lax.all_gather(w_out, "fsdp", axis=0, tiled=True),
        preferred_element_type=jnp.float32,
    )
    d_normed_out = d_normed_out + jnp.einsum(
        "rkq,kqi->ri", d_hidden_out, out_down, preferred_element_type=jnp.float32
    )
    d_mixed, d_gate = gate_pull(d_normed_out)
    d_x_mix, d_step_mix, d_b_mix, d_c_mix, d_state_in = mix_pull(
        d_mixed.reshape(streams, length, inner)
    )
    backward_carry = prefix(
        (through, d_state_in),
        "fsdp",
        pass_state,
        (jnp.ones_like(through), jnp.zeros_like(d_state_in)),
        True,
    )
    d_after = backward_carry[1]
    d_through = jnp.sum(d_after * state_in, axis=(2, 3))
    d_x_sum, d_step_sum, d_b_sum = summary_pull((d_through, d_after))
    d_conv_out = jnp.concatenate([d_x_mix + d_x_sum, d_b_mix + d_b_sum, d_c_mix], axis=2)
    (d_raw,) = step_pull(d_step_mix + d_step_sum)
    d_raw_low = d_raw.reshape(row_count, heads).astype(jnp.bfloat16)
    (d_extended,) = conv_pull(d_conv_out)
    spill_back = shifted(d_extended[:, : conv_taps - 1, :], "fsdp", -1)
    d_conv_in = d_extended[:, conv_taps - 1 :, :] + jnp.pad(
        spill_back, ((0, 0), (length - conv_taps + 1, 0), (0, 0))
    )
    d_proj = jnp.concatenate([d_gate, d_conv_in.reshape(row_count, conv_cols)], axis=1).astype(
        jnp.bfloat16
    )
    d_hidden_in = (
        jnp.einsum("rc,kqc->rkq", d_proj, in_up, preferred_element_type=jnp.float32)
        * onehot[:, :, None]
    ).astype(jnp.bfloat16)
    pieces = lax.all_gather((w_in, w_dt), "fsdp", axis=0, tiled=True)
    d_normed = jnp.einsum(
        "rc,dc->rd", d_proj, pieces[0], preferred_element_type=jnp.float32
    ) + jnp.einsum("rh,dh->rd", d_raw_low, pieces[1], preferred_element_type=jnp.float32)
    d_normed = d_normed + jnp.einsum(
        "rkq,kqd->rd", d_hidden_in, in_down, preferred_element_type=jnp.float32
    )
    (d_inputs,) = norm_pull(d_normed)
    input_grad = (grad_rows + d_inputs).reshape(1, streams, length, width)
    g_out_up = jnp.einsum(
        "rk,rd->kd",
        hidden_out.reshape(row_count, adapters * ranks),
        d_branch,
        preferred_element_type=jnp.float32,
    ).reshape(adapters, ranks, width)
    g_out_down = jnp.einsum(
        "rkq,ri->kqi", d_hidden_out, out_low, preferred_element_type=jnp.float32
    )
    g_in_up = jnp.einsum(
        "rk,rc->kc",
        hidden_in.reshape(row_count, adapters * ranks),
        d_proj,
        preferred_element_type=jnp.float32,
    ).reshape(adapters, ranks, in_cols)
    g_in_down = jnp.einsum(
        "rkq,rd->kqd", d_hidden_in, normed_low, preferred_element_type=jnp.float32
    )
    shares = (
        lax.psum_scatter(g_in_down, "fsdp", scatter_dimension=2, tiled=True),
        lax.psum_scatter(g_in_up, "fsdp", scatter_dimension=2, tiled=True),
        lax.psum_scatter(g_out_down, "fsdp", scatter_dimension=2, tiled=True),
        lax.psum_scatter(g_out_up, "fsdp", scatter_dimension=2, tiled=True),
    )
    totals = lax.psum((shares[0], shares[1], shares[2], shares[3]), "dp")
    return (block_output, input_grad, totals[0], totals[1], totals[2], totals[3])


def solution(mesh):
    in_specs = (
        P("dp", None, "fsdp", None),
        P("dp", None, None),
        P("dp", None, None),
        P(),
        P("fsdp", None),
        P("fsdp", None),
        P(),
        P(),
        P(),
        P(),
        P(),
        P(),
        P("fsdp", None),
        P(),
        P(),
        P(),
        P(),
        P("dp", None, "fsdp", None),
    )
    out_specs = (
        P("dp", None, "fsdp", None),
        P("dp", None, "fsdp", None),
        P(None, None, "fsdp"),
        P(None, None, "fsdp"),
        P(None, None, "fsdp"),
        P(None, None, "fsdp"),
    )
    return jax.shard_map(local, mesh=mesh, in_specs=in_specs, out_specs=out_specs, check_vma=False)
```

profile of v0, /device:TPU:0, one launch (start us, length us, event | category | flops | bytes accessed | tf_op | source)
XLA Modules:
  0.0 1184.4 jit_solution(29751481504098309)
XLA Ops:
  11.7 16.1 %all-gather.2 = bf16[8,192,48]{1,2,0:T(8,128)(2,1)S(1)} all-gather(bf16[1,192,48]{1,2,0:T(8,128)(2,1)} %bitcast.391), channel_id=1, replica_groups=mesh['dp'=4,'fsdp'=8] {'fsdp'}, dimensions={0}, use_global_device_ids=true | all-gather | bytes 165888 | tf_op jit(solution)/shard_map/all_gather | solution.py:179
  42.9 6.6 fusion.195
  49.5 137.8 %all-gather.8.cloned.1.call-done = bf16[1536,6400]{1,0:T(8,128)(2,1)} async-done(((bf16[192,6400]{1,0:T(8,128)(2,1)}), bf16[1536,6400]{1,0:T(8,128)(2,1)}) %all-gather.8.cloned.1.call-update) | async-done | bytes 19660816 | tf_op jit(solution)/shard_map/all_gather | solution.py:178
  187.3 20.2 %fusion.9 = bf16[512,6400]{1,0:T(8,128)(2,1)} fusion(f32[512,6400,1]{1,0,2:T(8,128)} %fusion.195, bf16[512,1536]{1,0:T(8,128)(2,1)S(1)} %copy-done.9, bf16[1536,6400]{1,0:T(8,128)(2,1)} %all-gather.8.cloned.1.call-done), kind=kOutput, calls=%fused_computation.16 | convolution fusion | flops 10072883200 | bytes 40894464 | tf_op jit(solution)/shard_map/dot_general | solution.py:182
  213.6 8.1 fusion.30
  221.7 6.2 slice.134
  227.9 6.6 copy.143
  234.6 8.9 fusion.55
  243.8 12.6 %all_gather.32 = f32[8,2,48]{2,1,0:T(2,128)S(1)} all-gather(f32[1,2,48]{2,1,0:T(2,128)S(1)} %bitcast_multiply_fusion.13), channel_id=1, replica_groups=mesh['dp'=4,'fsdp'=8] {'fsdp'}, dimensions={0}, use_global_device_ids=true | all-gather | bytes 3456 | tf_op jit(solution)/shard_map/all_gather | solution.py:20
  260.4 17.7 %all-gather.10.cloned.1.call-done = bf16[3072,1536]{1,0:T(8,128)(2,1)} async-done(((bf16[384,1536]{1,0:T(8,128)(2,1)}), bf16[3072,1536]{1,0:T(8,128)(2,1)}) %all-gather.10.cloned.1.call-update) | async-done | bytes 9437200 | tf_op jit(solution)/shard_map/all_gather | solution.py:248
  278.1 9.8 fusion.197
  290.4 208.6 %all-gather.12.cloned.1.call-done = f32[16,48,64,128]{3,2,1,0:T(8,128)} async-done(((f32[2,48,64,128]{3,2,1,0:T(8,128)}), f32[16,48,64,128]{3,2,1,0:T(8,128)}) %all-gather.12.cloned.1.call-update) | async-done | bytes 25165840 | tf_op jit(solution)/shard_map/all_gather | solution.py:20
  501.1 7.1 fusion.136
  511.0 41.6 %fusion.45 = f32[2,256,48,64]{1,3,2,0:T(8,128)} fusion(f32[2,256,48,64]{1,3,2,0:T(8,128)} %bitcast.362, f32[2,256,48,64]{1,3,2,0:T(8,128)S(1)} %fusion.136, f32[2,256,256]{2,1,0:T(8,128)S(1)} %copy-done.15, f32[2,48,256]{2,1,0:T(8,128)S(1)} %copy-done.25, pred[2,256,256]{2,1,0:T(8,128)(4,1)S(1)} %compare_and_fusion, f32[48]{0:T(128)S(1)} %copy-done.71, ...), kind=kOutput, calls=%fused_computation.74 | convolution fusion | flops 4858576896 | bytes 19824832 | tf_op jit(solution)/shard_map/jvp(slm,shlm,smhp->slhp)/dot_general | solution.py:115
  552.6 11.3 copy.192
  563.9 10.7 reshape.366
  574.6 11.7 multiply_reduce_fusion.2
  586.3 9.8 fusion.40
  596.1 6.7 copy.147
  602.8 8.4 reshape_reshape.3
  611.2 9.2 fusion.51
  628.5 5.1 reshape.364
  633.6 13.5 %fusion.111 = f32[2,256,128]{2,1,0:T(8,128)S(1)} fusion(f32[2,48,64,128]{3,2,1,0:T(8,128)} %get-tuple-element.134, f32[2,256,48,64]{1,0,3,2:T(2,128)} %reshape_reshape.3, f32[2,256,48]{1,2,0:T(8,128)S(1)} %copy-done.26), kind=kOutput, calls=%fused_computation.150 | convolution fusion | flops 2417491968 | bytes 9797632 | tf_op jit(solution)/shard_map/transpose(jvp(sln,shpn->slhp))/dot_general | solution.py:118
  647.1 23.5 %fusion.3 = f32[2,48,64,256]{3,2,1,0:T(8,128)} fusion(f32[2,256,256]{2,1,0:T(8,128)S(1)} %copy-done.16, f32[2,48,256]{2,1,0:T(8,128)S(1)} %copy-done.25, pred[2,256,256]{2,1,0:T(8,128)(4,1)S(1)} %compare_and_fusion, f32[2,48,256,64]{2,0,3,1:T(2,128)} %bitcast.368), kind=kOutput, calls=%fused_computation.11 | convolution fusion | flops 4850712576 | bytes 13336576 | tf_op jit(solution)/shard_map/transpose(jvp(slm,shlm,smhp->slhp))/dot_general | solution.py:115
  670.7 28.7 %fusion.1 = (f32[2,256,256]{2,1,0:T(8,128)S(1)}, f32[2,48,256,256]{3,2,1,0:T(8,128)}) fusion(f32[2,48,256]{2,1,0:T(8,128)S(1)} %copy-done.25, pred[2,256,256]{2,1,0:T(8,128)(4,1)S(1)} %compare_and_fusion, f32[2,256,48,64]{1,3,2,0:T(8,128)S(1)} %bitcast.367, f32[2,256,48]{1,2,0:T(8,128)S(1)} %copy-done.32, f32[2,48,256,64]{2,0,3,1:T(2,128)S(1)} %bitcast.371), kind=kOutput, calls=%fused_computation.8 | convolution fusion | flops 4858445824 | bytes 38600704 | tf_op jit(solution)/shard_map/transpose(jvp(slm,shlm,smhp->slhp))/dot_general | solution.py:115
  701.1 171.5 %all-gather.14.cloned.1.call-done = f32[16,48,64,128]{3,2,1,0:T(8,128)} async-done(((f32[2,48,64,128]{3,2,1,0:T(8,128)}), f32[16,48,64,128]{3,2,1,0:T(8,128)}) %all-gather.14.cloned.1.call-update) | async-done | bytes 25165840 | tf_op jit(solution)/shard_map/all_gather | solution.py:20
  874.7 34.3 %while.27 = (s32[]{:T(128)}, f32[2,48,64,128]{3,2,1,0:T(8,128)}, s32[]{:T(128)}, f32[8,2,48]{2,1,0:T(2,128)S(1)}, f32[8,2,48,64,128]{4,3,2,1,0:T(8,128)}, /*index=5*/s32[]{:T(128)}, s32[]{:T(128)}, s32[]{:T(128)}, s32[]{:T(128)}) while((s32[]{:T(128)}, f32[2,48,64,128]{3,2,1,0:T(8,128)}, s32[]{:T(128)}, f32[8,2,48]{2,1,0:T(2,128)S(1)}, ...), condition=%wide.region_10.11_spmd, body=%wide.region_9.10_spmd.sunk | while | flops 1572870 | bytes 9438491 | solution.py:29
  874.7 4.9 bitcast_add_fusion.8
  884.5 4.9 bitcast_add_fusion.8
  889.4 4.9 bitcast_add_fusion.8
  899.2 4.9 bitcast_add_fusion.8
  904.1 4.9 bitcast_add_fusion.8
  909.0 14.2 %fusion.108 = f32[2,256,128]{2,1,0:T(8,128)S(1)} fusion(f32[2,48,64,128]{3,2,1,0:T(8,128)} %get-tuple-element.135, f32[2,256,48,64]{1,3,2,0:T(8,128)} %bitcast.363, f32[2,256,48]{1,2,0:T(8,128)S(1)} %copy-done.24), kind=kOutput, calls=%fused_computation.149 | convolution fusion | flops 2417491968 | bytes 9797632 | tf_op jit(solution)/shard_map/transpose(jvp(slhp,sln,slh->shpn))/dot_general | solution.py:98
  923.2 15.6 %fusion.43 = (f32[2,256,48]{1,2,0:T(8,128)}, f32[2,256,48]{1,2,0:T(8,128)S(1)}, f32[2,256,48,64]{1,3,2,0:T(8,128)}, f32[2,256,48]{1,2,0:T(8,128)}) fusion(f32[2,256,48,64]{1,3,2,0:T(8,128)} %bitcast.364, f32[2,48,64,256]{3,2,1,0:T(8,128)} %fusion.3, f32[2,256,48]{1,2,0:T(8,128)S(1)} %copy-done.24, f32[2,256,48]{1,2,0:T(8,128)S(1)} %copy-done.32, ...), kind=kOutput, calls=%fused_computation.70 | convolution fusion | flops 2433146880 | bytes 35356864 | tf_op jit(solution)/shard_map/transpose(jvp(slhp,sln,slh->shpn))/dot_general | solution.py:98
  938.8 6.6 copy.158
  947.5 8.2 broadcast_multiply_fusion
  955.8 5.7 multiply_multiply_fusion.2
  965.6 7.8 pad_add_fusion
  984.8 5.1 reshape.360
  990.0 5.7 fusion.31
  995.6 13.7 %copy.188 = f32[8,16,6400]{1,0,2:T(8,128)} copy(f32[8,16,6400]{2,1,0:T(8,128)} %fusion.31) | data formatting | bytes 6553600
  1009.3 17.0 %reshape.362 = f32[6400,128]{1,0:T(8,128)} reshape(f32[6400,8,16]{2,1,0:T(8,128)} %bitcast.360) | data formatting | bytes 6553600
  1030.9 9.1 fusion.196
  1044.5 12.1 %fusion.8 = (f32[2,48,256]{2,1,0:T(8,128)}, f32[2,48,256]{2,1,0:T(8,128)}) fusion(f32[2,48,256,256]{3,2,1,0:T(8,128)S(1)} %bitcast.373, f32[2,256,256]{2,1,0:T(8,128)S(1)} %copy-done.17, f32[2,48,256]{2,1,0:T(8,128)S(1)} %copy-done.25, pred[2,256,256]{2,1,0:T(8,128)(4,1)S(1)} %copy-done.29), kind=kLoop, calls=%fused_computation.14 | loop fusion | flops 43991040 | bytes 26116096 | tf_op jit(solution)/shard_map/transpose(jvp())/reduce_sum | solution.py:110
  1070.3 5.7 reduce-window.26
  1077.9 6.3 reduce-window.24
  1092.3 17.4 %fusion.82 = (f32[512]{0:T(512)S(1)}, f32[512,1536]{1,0:T(8,128)}) fusion(bf16[1,2,256,1536]{3,2,1,0:T(8,128)(2,1)S(1)} %copy-done.6, f32[1536]{0:T(1024)S(1)} %copy-done.65, f32[512,1536]{1,0:T(8,128)} %convolution_bitcast_fusion, f32[512,1536]{1,0:T(8,128)S(1)} %fusion.198, bf16[1536,6400]{1,0:T(8,128)(2,1)} %all-gather.8.cloned.1.call-done, ...), kind=kOutput, calls=%fused_computation.125 | convolution fusion | flops 10084155392 | bytes 37232640 | tf_op jit(solution)/shard_map/rc,dc->rd/dot_general | solution.py:307
  1125.4 45.5 %all-reduce.10.cloned.1.call-done = (f32[8,16,192]{2,1,0:T(8,128)}, f32[8,16,800]{2,1,0:T(8,128)}, f32[8,16,384]{2,1,0:T(8,128)}, f32[8,16,192]{2,1,0:T(8,128)}) async-done(((f32[8,16,192]{2,1,0:T(8,128)}, f32[8,16,800]{2,1,0:T(8,128)}, f32[8,16,384]{2,1,0:T(8,128)}, f32[8,16,192]{2,1,0:T(8,128)}), (f32[8,16,192]{2,1,0:T(8,128)}, f32[8,16,800]{2,1,0:T(8,128)}, f32[8,16,384]{2,1,0:T(8,128)}, ...) | async-done | bytes 802832 | tf_op jit(solution)/shard_map/psum | solution.py:339
  (299 shorter events, 130.7 us)
Async XLA Ops:
  7.2 35.7 %copy-start = (bf16[8,16,6400]{2,1,0:T(8,128)(2,1)S(1)}, bf16[8,16,6400]{2,1,0:T(8,128)(2,1)}, u32[]{:S(2)}) copy-start(bf16[8,16,6400]{2,1,0:T(8,128)(2,1)} %param.36) | copy-start | bytes 4915204
  7.2 31.1 %copy-start.5 = (bf16[1,2,256,1536]{3,2,1,0:T(8,128)(2,1)S(1)}, bf16[1,2,256,1536]{3,2,1,0:T(8,128)(2,1)}, u32[]{:S(2)}) copy-start(bf16[1,2,256,1536]{3,2,1,0:T(8,128)(2,1)} %param.22) | copy-start | bytes 4718596
  7.2 23.7 %copy-start.72 = (f32[48]{0:T(128)S(1)}, f32[48]{0:T(128)}, u32[]{:S(2)}) copy-start(f32[48]{0:T(128)} %param.31) | copy-start | bytes 580
  7.2 180.1 %all-gather.8.cloned.1.call-start = ((), (), s32[]{:S(2)}) async-start(), calls=%async_computation.4 | async-start | bytes 22118400 | tf_op jit(solution)/shard_map/all_gather | solution.py:178
  7.9 270.2 %all-gather.10.cloned.1.call-start = ((), (), s32[]{:S(2)}) async-start(), calls=%async_computation.5 | async-start | bytes 10616832 | tf_op jit(solution)/shard_map/all_gather | solution.py:248
  8.7 490.4 %all-gather.12.cloned.1.call-start = ((), (), s32[]{:S(2)}) async-start(), calls=%async_computation.7 | async-start | bytes 28311552 | tf_op jit(solution)/shard_map/all_gather | solution.py:20
  11.7 37.8 %copy-start.52 = (f32[1,2,2,128]{3,1,2,0:T(2,128)}, f32[1,2,2,128]{3,1,2,0:T(2,128)S(1)}, u32[]{:S(2)}) copy-start(f32[1,2,2,128]{3,1,2,0:T(2,128)S(1)} %copy.201) | copy-start | bytes 6148
  11.7 37.8 %copy-start.54 = (f32[512]{0:T(512)}, f32[512]{0:T(512)S(1)}, u32[]{:S(2)}) copy-start(f32[512]{0:T(512)S(1)} %rsqrt.24) | copy-start | bytes 6148
  30.9 18.6 %copy-start.21 = (f32[2,256,48]{1,2,0:T(8,128)}, f32[2,256,48]{1,2,0:T(8,128)S(1)}, u32[]{:S(2)}) copy-start(f32[2,256,48]{1,2,0:T(8,128)S(1)} %get-tuple-element.206) | copy-start | bytes 294916
  30.9 18.6 %copy-start.47 = (u8[256,48]{0,1:T(8,128)(4,1)}, u8[256,48]{0,1:T(8,128)(4,1)S(1)}, u32[]{:S(2)}) copy-start(u8[256,48]{0,1:T(8,128)(4,1)S(1)} %get-tuple-element.205) | copy-start | bytes 36868
  34.0 15.5 %copy-start.11 = (f32[2,48,2,128]{3,1,2,0:T(8,128)}, f32[2,48,2,128]{3,1,2,0:T(8,128)S(1)}, u32[]{:S(2)}) copy-start(f32[2,48,2,128]{3,1,2,0:T(8,128)S(1)} %reduce-window.20) | copy-start | bytes 294916
  35.9 13.6 %copy-start.63 = (f32[2,48]{1,0:T(2,128)}, f32[2,48]{1,0:T(2,128)S(1)}, u32[]{:S(2)}) copy-start(f32[2,48]{1,0:T(2,128)S(1)} %get-tuple-element.142) | copy-start | bytes 1156
  36.6 177.0 %copy-start.56 = (f32[2,256]{1,0:T(2,128)}, f32[2,256]{1,0:T(2,128)S(1)}, u32[]{:S(2)}) copy-start(f32[2,256]{1,0:T(2,128)S(1)} %get-tuple-element.198) | copy-start | bytes 6148
  36.6 177.0 %copy-start.58 = (f32[2,256]{1,0:T(2,128)}, f32[2,256]{1,0:T(2,128)S(1)}, u32[]{:S(2)}) copy-start(f32[2,256]{1,0:T(2,128)S(1)} %get-tuple-element.199) | copy-start | bytes 6148
  36.6 177.0 %copy-start.60 = (f32[2,256]{1,0:T(2,128)}, f32[2,256]{1,0:T(2,128)S(1)}, u32[]{:S(2)}) copy-start(f32[2,256]{1,0:T(2,128)S(1)} %get-tuple-element.200) | copy-start | bytes 6148
  38.3 196.2 %copy-start.23 = (f32[2,256,48]{1,2,0:T(8,128)}, f32[2,256,48]{1,2,0:T(8,128)S(1)}, u32[]{:S(2)}) copy-start(f32[2,256,48]{1,2,0:T(8,128)S(1)} %get-tuple-element.190) | copy-start | bytes 294916
  42.9 144.4 %copy-start.9 = (bf16[512,1536]{1,0:T(8,128)(2,1)S(1)}, bf16[512,1536]{1,0:T(8,128)(2,1)}, u32[]{:S(2)}) copy-start(bf16[512,1536]{1,0:T(8,128)(2,1)} %copy-done.8) | copy-start | bytes 4718596
  209.8 3.1 collective-permute-start
  234.5 22.1 %copy-start.7 = (bf16[1,2,256,1536]{3,2,1,0:T(8,128)(2,1)S(1)}, bf16[1,2,256,1536]{3,2,1,0:T(8,128)(2,1)}, u32[]{:S(2)}) copy-start(bf16[1,2,256,1536]{3,2,1,0:T(8,128)(2,1)} %param.39) | copy-start | bytes 4718596
  234.6 23.5 %copy-start.75 = (f32[2,256,8]{1,2,0:T(8,128)S(1)}, f32[2,256,8]{1,2,0:T(8,128)}, u32[]{:S(2)}) copy-start(f32[2,256,8]{1,2,0:T(8,128)} %copy-done.74) | copy-start | bytes 49156
  243.5 629.1 %all-gather.14.cloned.1.call-start = ((), (), s32[]{:S(2)}) async-start(), calls=%async_computation.8 | async-start | bytes 28311552 | tf_op jit(solution)/shard_map/all_gather | solution.py:20
  243.5 44.4 %copy-start.67 = (f32[1,2,2,128]{3,1,2,0:T(2,128)}, f32[1,2,2,128]{3,1,2,0:T(2,128)S(1)}, u32[]{:S(2)}) copy-start(f32[1,2,2,128]{3,1,2,0:T(2,128)S(1)} %copy.202) | copy-start | bytes 6148
  243.7 12.7 %copy-start.69 = (f32[2]{0:T(128)}, f32[2]{0:T(128)S(1)}, u32[]{:S(2)}) copy-start(f32[2]{0:T(128)S(1)} %fusion.183) | copy-start | bytes 28
  256.6 414.0 %copy-start.28 = (pred[2,256,256]{2,1,0:T(8,128)(4,1)}, pred[2,256,256]{2,1,0:T(8,128)(4,1)S(1)}, u32[]{:S(2)}) copy-start(pred[2,256,256]{2,1,0:T(8,128)(4,1)S(1)} %compare_and_fusion) | copy-start | bytes 393220
  574.5 11.8 copy-start.4
  574.5 11.8 copy-start.64
  620.4 436.3 %reduce-scatter.17.cloned.1.call-start = ((), (), s32[]{:S(2)}) async-start(), calls=%async_computation.11 | async-start | bytes 884736
  633.6 13.5 %copy-start.16 = (f32[2,256,256]{2,1,0:T(8,128)S(1)}, f32[2,256,256]{2,1,0:T(8,128)}, u32[]{:S(2)}) copy-start(f32[2,256,256]{2,1,0:T(8,128)} %fusion.144) | copy-start | bytes 1572868
  633.6 37.0 %slice-start = ((s8[6291456]{0:T(1024)(128)(4,1)}), s8[4194304]{0:T(1024)(128)(4,1)S(1)}, s32[]{:S(2)}) async-start(s8[6291456]{0:T(1024)(128)(4,1)} %bitcast.365), calls=%async_computation.13 | async-start | bytes 8388608
  633.6 37.0 %slice-start.2 = ((s8[6291456]{0:T(1024)(128)(4,1)}), s8[4194304]{0:T(1024)(128)(4,1)S(1)}, s32[]{:S(2)}) async-start(s8[6291456]{0:T(1024)(128)(4,1)} %bitcast.369), calls=%async_computation.15 | async-start | bytes 8388608
  647.1 23.5 %slice-start.1 = ((s8[6291456]{0:T(1024)(128)(4,1)}), s8[2097152]{0:T(1024)(128)(4,1)S(1)}, s32[]{:S(2)}) async-start(s8[6291456]{0:T(1024)(128)(4,1)} %bitcast.365), calls=%async_computation.14 | async-start | bytes 4194304
  647.1 23.5 %slice-start.3 = ((s8[6291456]{0:T(1024)(128)(4,1)}), s8[2097152]{0:T(1024)(128)(4,1)S(1)}, s32[]{:S(2)}) async-start(s8[6291456]{0:T(1024)(128)(4,1)} %bitcast.369), calls=%async_computation.16 | async-start | bytes 4194304
  647.1 23.5 %copy-start.32 = (f32[2,256,48]{1,2,0:T(8,128)S(1)}, f32[2,256,48]{1,2,0:T(8,128)}, u32[]{:S(2)}) copy-start(f32[2,256,48]{1,2,0:T(8,128)} %get-tuple-element.189) | copy-start | bytes 294916
  699.5 410.3 %reduce-scatter.13.cloned.1.call-start = ((), (), s32[]{:S(2)}) async-start(), calls=%async_computation.9 | async-start | bytes 884736
  874.7 34.3 %copy-start.24 = (f32[2,256,48]{1,2,0:T(8,128)S(1)}, f32[2,256,48]{1,2,0:T(8,128)}, u32[]{:S(2)}) copy-start(f32[2,256,48]{1,2,0:T(8,128)} %copy-done.23) | copy-start | bytes 294916
  909.0 14.2 %copy-start.1 = (f32[2,48,64,128]{3,2,1,0:T(8,128)S(1)}, f32[2,48,64,128]{3,2,1,0:T(8,128)}, u32[]{:S(2)}) copy-start(f32[2,48,64,128]{3,2,1,0:T(8,128)} %get-tuple-element.135) | copy-start | bytes 9437188
  938.8 127.0 %copy-start.27 = (f32[2,256,48]{1,2,0:T(8,128)}, f32[2,256,48]{1,2,0:T(8,128)S(1)}, u32[]{:S(2)}) copy-start(f32[2,256,48]{1,2,0:T(8,128)S(1)} %get-tuple-element.139) | copy-start | bytes 294916
  964.3 9.1 collective-permute-start.1
  989.9 124.0 %reduce-scatter.15.cloned.1.call-start = ((), (), s32[]{:S(2)}) async-start(), calls=%async_computation.10 | async-start | bytes 3686400
  1009.3 17.1 %copy-start.19 = (bf16[8,192,48]{1,0,2:T(8,128)(2,1)S(1)}, bf16[8,192,48]{1,0,2:T(8,128)(2,1)}, u32[]{:S(2)}) copy-start(bf16[8,192,48]{1,0,2:T(8,128)(2,1)} %copy-done.18) | copy-start | bytes 442372
  1009.3 17.9 %copy-start.43 = (bf16[512,8,16]{0,2,1:T(8,128)(2,1)S(1)}, bf16[512,8,16]{0,2,1:T(8,128)(2,1)}, u32[]{:S(2)}) copy-start(bf16[512,8,16]{0,2,1:T(8,128)(2,1)} %fusion.117) | copy-start | bytes 393220
  1026.3 94.2 %reduce-scatter.11.cloned.1.call-start = ((), (), s32[]{:S(2)}) async-start(), calls=%async_computation.6 | async-start | bytes 1769472 | tf_op jit(solution)/shard_map/reduce_scatter | solution.py:336
  1030.9 11.0 slice-start.4
  1030.9 11.0 slice-start.5
  1030.9 11.0 slice-start.6
  1030.9 11.0 slice-start.7
  1030.9 12.1 %slice-start.8 = ((s8[25165824]{0:T(1024)(128)(4,1)}), s8[4194304]{0:T(1024)(128)(4,1)S(1)}, s32[]{:S(2)}) async-start(s8[25165824]{0:T(1024)(128)(4,1)} %bitcast.372), calls=%async_computation.21 | async-start | bytes 8388608
  1056.6 114.3 %all-reduce.10.cloned.1.call-start = ((), (), s32[]{:S(2)}) async-start(), calls=%async_computation.12 | async-start | bytes 1835008 | tf_op jit(solution)/shard_map/psum | solution.py:339
  (50 other events, 320.2 us)
Sparse Core Ops, SparseCore 0:
  9.7 177.5 all-gather.7
  189.0 89.1 all-gather.9
  280.3 218.6 all-gather.11
  620.5 252.0 all-gather.13
  874.7 29.8 reduce-scatter.16
  990.0 30.4 reduce-scatter.12
  1026.5 40.2 reduce-scatter.14
  1069.1 33.0 reduce-scatter.10
  1120.6 50.1 all-reduce.9
where the time goes:
time: 1190 us; the launch traced here: 1180 us
  waiting for transfers between devices  583 us (49%)
  matrix products  273 us (23%)
  local copies, waits for them, and re-layouts  150 us (13%)
  other arithmetic  131 us (11%)
  blocking collectives  28.7 us (2%)
  between operations  15.4 us (1%)
    all_gather x2, waiting for transfers between devices, prefix(): gathered = jax.tree.map(lambda a: lax.all_gather(a, axis), part)  380 us
    all_gather x1, waiting for transfers between devices, local(): lax.all_gather(w_in, 'fsdp', axis=0, tiled=True)  138 us
    dot_general x3, matrix products, span_mix(): jnp.einsum('slm,shlm,smhp->slhp', c_dot_b, decay_mat, scaled_x, precision...  93.8 us
    unnamed x194, local copies, waits for them, and re-layouts  82.9 us
    psum x1, waiting for transfers between devices, local(): totals = lax.psum((shares[0], shares[1], shares[2], shares[3]), 'dp')  45.5 us
    dot_general x3, matrix products, span_summary(): jnp.einsum('slhp,sln,slh->shpn', heads_x, input_b, weight, precision=HIGH...  38.7 us
    add x7, other arithmetic, pass_state(): later_part[0][:, :, None, None] * earlier[1] + later_part[1]  34.3 us
    another operation x11, other arithmetic  32.2 us
  transfers between devices with their start and end apart: 11, of which 6 were waited for; matrix products, arithmetic and copies ran while one was open for 35% of the time, Pallas kernels for 0%

commit v1 on v0

v1 whole, which is shorter than its diff:
```python
import functools

import jax
import jax.numpy as jnp
from jax import lax
from jax.experimental import pallas as pl
from jax.experimental.pallas import tpu as pltpu
from jax.sharding import PartitionSpec as P

EPSILON = 1e-05
HIGHEST = lax.Precision.HIGHEST
F32, LOW = jnp.float32, jnp.bfloat16
HALO = 16
LANES = 128
BLOCK = 256
VMEM = 48 * 1024 * 1024


def dot(a, b, precision=None):
    return lax.dot_general(
        a, b, (((1,), (0,)), ((), ())), precision=precision, preferred_element_type=F32
    )


def dot_nt(a, b, precision=None):
    return lax.dot_general(
        a, b, (((1,), (1,)), ((), ())), precision=precision, preferred_element_type=F32
    )


def iota(shape, dim):
    return lax.broadcasted_iota(jnp.int32, shape, dim)


def expand(values, spread, terms):
    total, rest = None, values
    for _ in range(terms):
        part = rest.astype(LOW)
        rest = rest - part.astype(F32)
        got = dot(part, spread)
        total = got if total is None else total + got
    return total


def sigmoid(v):
    return 1.0 / (1.0 + jnp.exp(-v))


def core_at(groups, streams, slots):
    return groups + 1 + streams * slots


class Meta:
    def __init__(self, ref, groups, slots):
        self.ref, self.groups, self.slots = ref, groups, slots

    def first(self):
        return self.ref[self.groups]

    def core(self, streams):
        return self.ref[core_at(self.groups, streams, self.slots)]

    def end(self, stream, slot):
        return self.ref[self.groups + 1 + stream * self.slots + slot]

    def segment(self, stream, pos):
        seg = jnp.zeros_like(pos)
        for slot in range(self.slots):
            seg = seg + (pos >= self.end(stream, slot)).astype(jnp.int32)
        return jnp.where(pos < 0, -1, seg)

    def scalar_segment(self, stream, pos):
        seg = jnp.int32(0)
        for slot in range(self.slots):
            seg = seg + jnp.where(pos >= self.end(stream, slot), 1, 0)
        return jnp.where(pos < 0, -1, seg)


def tap_masks(meta, stream, taps, length):
    pos = meta.first() + iota((length, LANES), 0)
    own = meta.segment(stream, pos)
    masks = []
    for k in range(taps - 1):
        masks.append((meta.segment(stream, pos - (taps - 1 - k)) == own).astype(F32))
    return masks


def wide(mask, cols):
    return jnp.concatenate([mask] * (cols // LANES), axis=1)


def conv_pre(block, masks, cw, cb):
    taps, cols = cw.shape
    total = cb + cw[taps - 1 : taps] * block[HALO:]
    for k in range(taps - 1):
        moved = pltpu.roll(block, taps - 1 - k, 0)[HALO:]
        total = total + cw[k : k + 1] * moved * wide(masks[k], cols)
    return total


def conv_back(d_out, block, masks, cw, cb):
    taps, cols = cw.shape
    pre = conv_pre(block, masks, cw, cb)
    sig = sigmoid(pre)
    d_pre = d_out * (sig * (1.0 + pre * (1.0 - sig)))
    total = jnp.concatenate([jnp.zeros((HALO, cols), F32), cw[taps - 1 : taps] * d_pre], axis=0)
    rows = total.shape[0]
    for k in range(taps - 1):
        part = cw[k : k + 1] * d_pre * wide(masks[k], cols)
        part = jnp.concatenate([jnp.zeros((HALO, cols), F32), part], axis=0)
        total = total + pltpu.roll(part, rows - (taps - 1 - k), 0)
    return total


def spread_of(first_head, cols, per_head):
    head = lax.shift_right_logical(iota((LANES, cols), 1), per_head.bit_length() - 1) + first_head
    return (iota((LANES, cols), 0) == head).astype(LOW)


def gather_of(first_head, cols, per_head):
    head = lax.shift_right_logical(iota((cols, LANES), 0), per_head.bit_length() - 1) + first_head
    return (iota((cols, LANES), 1) == head).astype(LOW)


def sum_heads(values, gather):
    part = values.astype(LOW)
    rest = (values - part.astype(F32)).astype(LOW)
    return dot(part, gather) + dot(rest, gather)


def halves_product(nx, hx, w_mine, w_other, up, core):
    return (
        dot(nx[core], w_mine[...]) + dot(nx[1 - core], w_other[...]) + dot(hx[...], up[...])
    ).astype(LOW)


def gate_project_kernel(cfg, meta_ref, nx, hx, w_mine, w_other, up, out):
    streams, length, slots, groups, per_group, headdim = cfg
    core = meta_ref[core_at(groups, streams, slots)]
    out[...] = halves_product(nx, hx, w_mine, w_other, up, core)


def half_specs(cfg, weights, cols):
    streams, length, slots, groups, per_group, headdim = cfg
    core = core_at(groups, streams, slots)
    mine, other = weights
    if mine is other:
        half = mine.shape[0] // 2
        return [
            pl.BlockSpec((half, cols), lambda i, m: (m[core], i)),
            pl.BlockSpec((half, cols), lambda i, m: (1 - m[core], i)),
        ]
    return [pl.BlockSpec((mine.shape[0], cols), lambda i, m: (0, i))] * 2


def gate_project(cfg, meta, slot, nx, hx, weights, in_up):
    cols = weights[0].shape[1]
    rows = nx.shape[1]
    blocks = cols // BLOCK
    return pl.pallas_call(
        functools.partial(gate_project_kernel, cfg),
        grid_spec=pltpu.PrefetchScalarGridSpec(
            num_scalar_prefetch=1, grid=(blocks,),
            in_specs=[
                pl.BlockSpec(nx.shape, lambda i, m: (0, 0, 0)),
                pl.BlockSpec(hx.shape, lambda i, m: (0, 0)),
                *half_specs(cfg, weights, BLOCK),
                pl.BlockSpec((in_up.shape[0], BLOCK), lambda i, m: (0, m[slot] * blocks + i)),
            ],
            out_specs=pl.BlockSpec((rows, BLOCK), lambda i, m: (0, i)),
        ),
        out_shape=jax.ShapeDtypeStruct((rows, cols), LOW),
        compiler_params=pltpu.CompilerParams(vmem_limit_bytes=VMEM),
        cost_estimate=pl.CostEstimate(
            flops=2 * rows * (2 * nx.shape[2] + 256) * cols, bytes_accessed=6 * nx.shape[2] * cols, transcendentals=0
        ),
        name="project_gate",
    )(meta, nx, hx, *weights, in_up)


def project_kernel(cfg, slot, with_state, meta_ref, nx, hx, w_mine, w_other, up, cw, cb, *rest):
    streams, length, slots, groups, per_group, headdim = cfg
    meta = Meta(meta_ref, groups, slots)
    if with_state:
        weight, bt, ci, x_out, state = rest
        per_block = BLOCK // headdim
        first_head = meta_ref[slot] * per_group + pl.program_id(0) * per_block
        spread = spread_of(first_head, BLOCK, headdim)
    else:
        ci, x_out = rest
    low = halves_product(nx, hx, w_mine, w_other, up, meta.core(streams))
    ci[...] = low
    full = low.astype(F32)
    for s in range(streams):
        block = full[s * (HALO + length) : (s + 1) * (HALO + length)]
        masks = tap_masks(meta, s, cw.shape[0], length)
        pre = conv_pre(block, masks, cw[...], cb[...])
        x = pre * sigmoid(pre)
        x_out[s * length : (s + 1) * length] = x
        if with_state:
            scale = expand(weight[s * length : (s + 1) * length], spread, 2)
            state[s] = dot(bt[s], (x * scale).astype(LOW)).astype(LOW)


def project(cfg, meta, slot, nx, hx, weights, in_up, conv_weight, conv_bias, first_block, blocks, weight=None, bt=None):
    streams, length, slots, groups, per_group, headdim = cfg
    rows = streams * length
    ext = nx.shape[1]
    with_state = weight is not None
    gate_blocks = (in_up.shape[1] - conv_weight.shape[1]) // BLOCK

    def place(i, m):
        return first_block + (m[slot] * blocks if with_state else 0) + i

    whole = lambda i, m: (0, 0)
    own = lambda i, m: (0, i)
    conv_at = lambda i, m: (0, place(i, m))
    in_specs = [
        pl.BlockSpec(nx.shape, lambda i, m: (0, 0, 0)),
        pl.BlockSpec(hx.shape, whole),
        *half_specs(cfg, weights, BLOCK),
        pl.BlockSpec((in_up.shape[0], BLOCK), lambda i, m: (0, gate_blocks + place(i, m))),
        pl.BlockSpec((conv_weight.shape[0], BLOCK), conv_at),
        pl.BlockSpec((1, BLOCK), conv_at),
    ]
    args = [nx, hx, *weights, in_up, conv_weight, conv_bias]
    out_specs = [pl.BlockSpec((ext, BLOCK), own), pl.BlockSpec((rows, BLOCK), own)]
    cols = blocks * BLOCK
    out_shape = [jax.ShapeDtypeStruct((ext, cols), LOW), jax.ShapeDtypeStruct((rows, cols), F32)]
    if with_state:
        args += [weight, bt]
        in_specs += [
            pl.BlockSpec(weight.shape, whole),
            pl.BlockSpec(bt.shape, lambda i, m: (0, 0, 0)),
        ]
        out_specs.append(pl.BlockSpec((streams, bt.shape[1], BLOCK), lambda i, m: (0, 0, i)))
        out_shape.append(jax.ShapeDtypeStruct((streams, bt.shape[1], cols), LOW))
    return pl.pallas_call(
        functools.partial(project_kernel, cfg, slot, with_state),
        grid_spec=pltpu.PrefetchScalarGridSpec(
            num_scalar_prefetch=1, grid=(blocks,), in_specs=in_specs, out_specs=out_specs
        ),
        out_shape=out_shape,
        compiler_params=pltpu.CompilerParams(vmem_limit_bytes=VMEM),
        cost_estimate=pl.CostEstimate(
            flops=2 * ext * (2 * nx.shape[2] + 256) * cols,
            bytes_accessed=4 * nx.shape[2] * cols + ext * cols * 8,
            transcendentals=rows * cols,
        ),
        name="project_conv",
    )(meta, *args)


def decay_kernel(cfg, state_size, meta_ref, step, rates, bc, log_d, enter_d, rest_d, weight, log_t, through, g, gt, b_low, c_low, bt, ct):
    streams, length, slots, groups, per_group, headdim = cfg
    meta = Meta(meta_ref, groups, slots)
    first = meta.first()
    lower = (iota((length, length), 0) >= iota((length, length), 1)).astype(F32)
    per_block = BLOCK // headdim
    for s in range(streams):
        at = slice(s * length, (s + 1) * length)
        prior = meta.scalar_segment(s, first - 1)
        last = meta.scalar_segment(s, first + length - 1)
        seg = meta.segment(s, first + iota((length, LANES), 0))
        seg_u = meta.segment(s, first + iota((length, length), 1))
        seg_t = meta.segment(s, first + iota((length, length), 0))
        st = step[at]
        logs = dot(lower, -st * rates[...], HIGHEST)
        log_d[at] = logs
        enter_d[at] = jnp.where(seg == prior, jnp.exp(logs), 0.0)
        remain = jnp.where(seg == last, jnp.exp(logs[length - 1 : length] - logs), 0.0)
        rest_d[at] = remain
        weight[at] = remain * st
        through[s] = jnp.broadcast_to(
            jnp.where(prior == last, jnp.exp(logs[length - 1 : length]), 0.0), (8, LANES)
        )
        turned = jnp.transpose(logs)
        for b in range(log_t.shape[1]):
            log_t[s, b, 0:per_block] = turned[b * per_block : (b + 1) * per_block]
        b_in, c_in = bc[at, :state_size], bc[at, state_size:]
        pairs = jnp.where(seg_u == seg_t, lower, 0.0) * dot_nt(c_in, b_in, HIGHEST)
        g[s] = pairs
        gt[s] = jnp.transpose(pairs)
        b_low[at] = b_in.astype(LOW)
        c_low[at] = c_in.astype(LOW)
        bt[s] = jnp.transpose(b_in).astype(LOW)
        ct[s] = jnp.transpose(c_in).astype(LOW)


def decays(cfg, meta, step, rates, bc, heads):
    streams, length, slots, groups, per_group, headdim = cfg
    rows = streams * length
    state_size = bc.shape[1] // 2
    blocks = heads * headdim // BLOCK
    row = lambda dtype, cols: jax.ShapeDtypeStruct((rows, cols), dtype)
    cube = lambda dtype, a, b: jax.ShapeDtypeStruct((streams, a, b), dtype)
    outs = [
        row(F32, LANES), row(F32, LANES), row(F32, LANES), row(F32, LANES),
        jax.ShapeDtypeStruct((streams, blocks, 8, length), F32),
        cube(F32, 8, LANES),
        cube(F32, length, length), cube(F32, length, length),
        row(LOW, state_size), row(LOW, state_size),
        cube(LOW, state_size, length), cube(LOW, state_size, length),
    ]
    zeros = lambda n: (lambda i, m: (0,) * n)
    return pl.pallas_call(
        functools.partial(decay_kernel, cfg, state_size),
        grid_spec=pltpu.PrefetchScalarGridSpec(
            num_scalar_prefetch=1, grid=(1,),
            in_specs=[pl.BlockSpec(a.shape, zeros(a.ndim)) for a in (step, rates, bc)],
            out_specs=[pl.BlockSpec(a.shape, zeros(len(a.shape))) for a in outs],
        ),
        out_shape=outs,
        compiler_params=pltpu.CompilerParams(vmem_limit_bytes=VMEM),
        name="decays",
    )(meta, step, rates, bc)


def inside_kernel(cfg, slot, meta_ref, x, step, logs, log_t, g, y):
    streams, length, slots, groups, per_group, headdim = cfg
    per_block = BLOCK // headdim
    first_head = meta_ref[slot] * per_group + pl.program_id(0) * per_block
    spread = spread_of(first_head, BLOCK, headdim)
    columns = spread_of(first_head, per_block * LANES, LANES)
    half = length // 2
    left = iota((length, LANES), 1) < headdim
    for s in range(streams):
        at = slice(s * length, (s + 1) * length)
        log_col = expand(logs[at], columns, 3)
        xs = (x[at] * expand(step[at], spread, 2)).astype(LOW)
        for pair in range(per_block // 2):
            cols = slice(pair * LANES, (pair + 1) * LANES)
            got = []
            for h in (2 * pair, 2 * pair + 1):
                col = log_col[:, h * LANES : (h + 1) * LANES]
                row = log_t[s, 0, h : h + 1]
                top = jnp.exp(jnp.minimum(col[:half] - row[:, :half], 0.0)) * g[s, :half, :half]
                low = jnp.exp(jnp.minimum(wide(col[half:], length) - row, 0.0)) * g[s, half:]
                got.append(
                    jnp.concatenate(
                        [dot(top.astype(LOW), xs[:half, cols]), dot(low.astype(LOW), xs[:, cols])], axis=0
                    )
                )
            y[at, cols] = jnp.where(left, got[0], got[1])


def inside(cfg, meta, slot, x, step, logs, log_t, g):
    streams, length, slots, groups, per_group, headdim = cfg
    blocks = x.shape[1] // BLOCK
    whole = lambda i, m: (0, 0)
    own = pl.BlockSpec((x.shape[0], BLOCK), lambda i, m: (0, i))
    return pl.pallas_call(
        functools.partial(inside_kernel, cfg, slot),
        grid_spec=pltpu.PrefetchScalarGridSpec(
            num_scalar_prefetch=1, grid=(blocks,),
            in_specs=[
                own,
                pl.BlockSpec(step.shape, whole),
                pl.BlockSpec(logs.shape, whole),
                pl.BlockSpec((streams, 1, 8, length), lambda i, m: (0, m[slot] * blocks + i, 0, 0)),
                pl.BlockSpec(g.shape, lambda i, m: (0, 0, 0)),
            ],
            out_specs=own,
        ),
        out_shape=jax.ShapeDtypeStruct(x.shape, F32),
        compiler_params=pltpu.CompilerParams(vmem_limit_bytes=VMEM),
        cost_estimate=pl.CostEstimate(
            flops=8 * x.shape[0] * length * x.shape[1], bytes_accessed=x.size * 8, transcendentals=4 * x.size
        ),
        name="inside",
    )(meta, x, step, logs, log_t, g)


def gate_kernel(cfg, meta_ref, *refs):
    streams, length, slots, groups, per_group, headdim = cfg
    xs, ys, states, gates = (refs[i * groups : (i + 1) * groups] for i in range(4))
    refs = refs[4 * groups :]
    d_out, enter_d, c_low, ct, skip, gain = refs[:6]
    out_low, d_mixed, d_gate, row_sum, d_state, y_all, v_all = refs[6:]
    width = per_group * headdim
    inner = groups * width
    rows = d_out.shape[0]
    per_stream = length // rows
    entering = enter_d[...]
    squares = jnp.zeros((rows, LANES), F32)
    crossed = jnp.zeros((rows, LANES), F32)

    def fold(values):
        total = values[:, :LANES]
        for j in range(1, values.shape[1] // LANES):
            total = total + values[:, j * LANES : (j + 1) * LANES]
        return total

    for j in range(groups):
        place = meta_ref[j]
        cols = pl.ds(pl.multiple_of(place * width, width), width)
        spread = spread_of(place * per_group, width, headdim)
        scale = expand(entering, spread, 2)
        y = ys[j][...] + dot(c_low[...], states[j][0]) * scale
        y_all[:, cols] = y
        gated = gates[j][...].astype(F32)
        v = (y + skip[:, cols] * xs[j][...]) * (gated * sigmoid(gated))
        v_all[:, cols] = v
        squares = squares + fold(v * v)
        crossed = crossed + fold(v * d_out[:, cols] * gain[:, cols])
    mean_sq = jnp.sum(squares, axis=1, keepdims=True) / inner
    rs = lax.rsqrt(mean_sq + EPSILON)
    mean_cross = jnp.sum(crossed, axis=1, keepdims=True) / inner
    pull = rs * rs * rs * mean_cross
    sums = jnp.zeros((rows, LANES), F32)
    fresh = pl.program_id(0) % per_stream == 0
    for j in range(groups):
        place = meta_ref[j]
        cols = pl.ds(pl.multiple_of(place * width, width), width)
        spread = spread_of(place * per_group, width, headdim)
        gated = gates[j][...].astype(F32)
        sig = sigmoid(gated)
        v = v_all[:, cols]
        y = y_all[:, cols]
        out_low[:, cols] = (v * rs * gain[:, cols]).astype(LOW)
        d_v = rs * d_out[:, cols] * gain[:, cols] - v * pull
        dm = d_v * (gated * sig)
        d_mixed[:, cols] = dm
        mixed = y + skip[:, cols] * xs[j][...]
        d_gate[:, cols] = (d_v * mixed * (sig * (1.0 + gated * (1.0 - sig)))).astype(LOW)
        sums = sums + sum_heads(
            dm.astype(LOW).astype(F32) * y, gather_of(place * per_group, width, headdim)
        )
        part = dot(ct[0], (dm * expand(entering, spread, 2)).astype(LOW))

        @pl.when(fresh)
        def _():
            d_state[0, :, cols] = part

        @pl.when(jnp.logical_not(fresh))
        def _():
            d_state[0, :, cols] += part

    row_sum[...] = sums


def gated(cfg, meta, xs, ys, states, gates, d_out, enter_d, c_low, ct, skip, gain):
    streams, length, slots, groups, per_group, headdim = cfg
    rows = 128
    per_stream = length // rows
    width = xs[0].shape[1]
    inner = d_out.shape[1]
    state_size = c_low.shape[1]
    total = streams * length
    row = lambda cols: pl.BlockSpec((rows, cols), lambda i, m: (i, 0))
    state = pl.BlockSpec((1, state_size, width), lambda i, m: (i // per_stream, 0, 0))
    flat = pl.BlockSpec((1, inner), lambda i, m: (0, 0))
    return pl.pallas_call(
        functools.partial(gate_kernel, cfg),
        grid_spec=pltpu.PrefetchScalarGridSpec(
            num_scalar_prefetch=1, grid=(total // rows,),
            in_specs=[row(width)] * (2 * groups) + [state] * groups + [row(width)] * groups
            + [
                row(inner), row(LANES), row(state_size),
                pl.BlockSpec((1, state_size, rows), lambda i, m: (i // per_stream, 0, i % per_stream)),
                flat, flat,
            ],
            out_specs=[
                row(inner), row(inner), row(inner), row(LANES),
                pl.BlockSpec((1, state_size, inner), lambda i, m: (i // per_stream, 0, 0)),
            ],
            scratch_shapes=[pltpu.VMEM((rows, inner), F32), pltpu.VMEM((rows, inner), F32)],
        ),
        out_shape=[
            jax.ShapeDtypeStruct((total, inner), LOW),
            jax.ShapeDtypeStruct((total, inner), F32),
            jax.ShapeDtypeStruct((total, inner), LOW),
            jax.ShapeDtypeStruct((total, LANES), F32),
            jax.ShapeDtypeStruct((streams, state_size, inner), F32),
        ],
        compiler_params=pltpu.CompilerParams(vmem_limit_bytes=VMEM),
        name="gated",
    )(meta, *xs, *ys, *states, *gates, d_out, enter_d, c_low, ct, skip, gain)


def inside_back_kernel(cfg, slot, meta_ref, x, d_mixed, step, logs, enter_d, log_t, gt, state, dxs, dgt, dc):
    streams, length, slots, groups, per_group, headdim = cfg
    per_block = BLOCK // headdim
    first_head = meta_ref[slot] * per_group + pl.program_id(0) * per_block
    spread = spread_of(first_head, BLOCK, headdim)
    columns = spread_of(first_head, per_block * LANES, LANES)
    half = length // 2
    left = iota((length, LANES), 1) < headdim

    @pl.when(pl.program_id(0) == 0)
    def _():
        dgt[...] = jnp.zeros_like(dgt)
        dc[...] = jnp.zeros_like(dc)

    for s in range(streams):
        at = slice(s * length, (s + 1) * length)
        log_col = expand(logs[at], columns, 3)
        xs = (x[at] * expand(step[at], spread, 2)).astype(LOW)
        dm = d_mixed[at]
        dm_low = dm.astype(LOW)
        dc[at] += dot_nt((dm * expand(enter_d[at], spread, 2)).astype(LOW), state[s])
        sum_top, sum_low = None, None
        for pair in range(per_block // 2):
            cols = slice(pair * LANES, (pair + 1) * LANES)
            got = []
            for h in (2 * pair, 2 * pair + 1):
                col = log_col[:, h * LANES : (h + 1) * LANES]
                row = log_t[s, 0, h : h + 1]
                top = jnp.exp(jnp.minimum(row - wide(col[:half], length), 0.0))
                low = jnp.exp(jnp.minimum(row[:, half:] - col[half:], 0.0))
                k_top = (top * gt[s, :half]).astype(LOW)
                k_low = (low * gt[s, half:, half:]).astype(LOW)
                got.append(
                    jnp.concatenate([dot(k_top, dm_low[:, cols]), dot(k_low, dm_low[half:, cols])], axis=0)
                )
                mine = left if h % 2 == 0 else jnp.logical_not(left)
                x_mine = jnp.where(mine, xs[:, cols], jnp.zeros_like(xs[:, cols]))
                add_top = dot_nt(x_mine[:half], dm_low[:, cols]) * top
                add_low = dot_nt(x_mine[half:], dm_low[half:, cols]) * low
                sum_top = add_top if sum_top is None else sum_top + add_top
                sum_low = add_low if sum_low is None else sum_low + add_low
            dxs[at, cols] = jnp.where(left, got[0], got[1])
        dgt[s, :half] += sum_top
        dgt[s, half:, half:] += sum_low


def inside_back(cfg, meta, slot, x, d_mixed, step, logs, enter_d, log_t, gt, state):
    streams, length, slots, groups, per_group, headdim = cfg
    blocks = x.shape[1] // BLOCK
    state_size = state.shape[1]
    whole = lambda i, m: (0, 0)
    cube = lambda i, m: (0, 0, 0)
    own = pl.BlockSpec((x.shape[0], BLOCK), lambda i, m: (0, i))
    return pl.pallas_call(
        functools.partial(inside_back_kernel, cfg, slot),
        grid_spec=pltpu.PrefetchScalarGridSpec(
            num_scalar_prefetch=1, grid=(blocks,),
            in_specs=[
                own,
                pl.BlockSpec((x.shape[0], BLOCK), lambda i, m: (0, m[slot] * blocks + i)),
                pl.BlockSpec(step.shape, whole),
                pl.BlockSpec(logs.shape, whole),
                pl.BlockSpec(enter_d.shape, whole),
                pl.BlockSpec((streams, 1, 8, length), lambda i, m: (0, m[slot] * blocks + i, 0, 0)),
                pl.BlockSpec(gt.shape, cube),
                pl.BlockSpec((streams, state_size, BLOCK), lambda i, m: (0, 0, i)),
            ],
            out_specs=[own, pl.BlockSpec(gt.shape, cube), pl.BlockSpec((x.shape[0], state_size), whole)],
        ),
        out_shape=[
            jax.ShapeDtypeStruct(x.shape, F32),
            jax.ShapeDtypeStruct(gt.shape, F32),
            jax.ShapeDtypeStruct((x.shape[0], state_size), F32),
        ],
        compiler_params=pltpu.CompilerParams(vmem_limit_bytes=VMEM),
        cost_estimate=pl.CostEstimate(
            flops=16 * x.shape[0] * length * x.shape[1], bytes_accessed=x.size * 12, transcendentals=4 * x.size
        ),
        name="inside_back",
    )(meta, x, d_mixed, step, logs, enter_d, log_t, gt, state)


def after_kernel(cfg, slot, meta_ref, x, d_mixed, dxs, d_after, state, step, rest_d, b_low, skip, ci, cw, cb, dci, tail, spill, direct, sums, db):
    streams, length, slots, groups, per_group, headdim = cfg
    meta = Meta(meta_ref, groups, slots)
    per_block = BLOCK // headdim
    first_head = meta_ref[slot] * per_group + pl.program_id(0) * per_block
    spread = spread_of(first_head, BLOCK, headdim)
    gather = gather_of(first_head, BLOCK, headdim)

    @pl.when(pl.program_id(0) == 0)
    def _():
        direct[...] = jnp.zeros_like(direct)
        sums[...] = jnp.zeros_like(sums)
        db[...] = jnp.zeros_like(db)

    for s in range(streams):
        at = slice(s * length, (s + 1) * length)
        st = step[at]
        remain = rest_d[at]
        x_s = x[at]
        step_wide = expand(st, spread, 2)
        back = expand(remain, spread, 2) * dot(b_low[at], d_after[s])
        inner_back = dxs[at]
        x_weighted = x_s * expand(remain * st, spread, 2)
        db[at] += dot_nt(x_weighted.astype(LOW), d_after[s])
        from_after = sum_heads(x_s * back, gather)
        direct[at] += sum_heads(x_s * inner_back, gather) + from_after
        crossed = jnp.sum(d_after[s].astype(F32) * state[s].astype(F32), axis=0, keepdims=True)
        crossed = sum_heads(jnp.broadcast_to(crossed, (8, BLOCK)), gather)
        after_sum = jnp.broadcast_to(jnp.sum(from_after * st, axis=0, keepdims=True), (8, LANES))
        sums[s] += jnp.where(iota((8, LANES), 0) == 0, crossed, after_sum)
        d_x = step_wide * (inner_back + back) + skip[...] * d_mixed[at]
        block = ci[s * (HALO + length) : (s + 1) * (HALO + length)].astype(F32)
        masks = tap_masks(meta, s, cw.shape[0], length)
        total = conv_back(d_x, block, masks, cw[...], cb[...])
        dci[at] = total[HALO:].astype(LOW)
        tail[s] = total[HALO + length - 8 :]
        spill[s] = total[HALO - 8 : HALO]


def after(cfg, meta, slot, x, d_mixed, dxs, d_after, state, step, rest_d, b_low, skip, ci, conv_weight, conv_bias):
    streams, length, slots, groups, per_group, headdim = cfg
    blocks = x.shape[1] // BLOCK
    state_size = state.shape[1]
    rows = x.shape[0]
    whole = lambda i, m: (0, 0)
    own = pl.BlockSpec((rows, BLOCK), lambda i, m: (0, i))
    placed = lambda r: pl.BlockSpec((r, BLOCK), lambda i, m: (0, m[slot] * blocks + i))
    cube = lambda r: pl.BlockSpec((streams, r, BLOCK), lambda i, m: (0, 0, i))
    return pl.pallas_call(
        functools.partial(after_kernel, cfg, slot),
        grid_spec=pltpu.PrefetchScalarGridSpec(
            num_scalar_prefetch=1, grid=(blocks,),
            in_specs=[
                own, placed(rows), own, cube(state_size), cube(state_size),
                pl.BlockSpec(step.shape, whole), pl.BlockSpec(rest_d.shape, whole), pl.BlockSpec(b_low.shape, whole),
                placed(1), pl.BlockSpec((ci.shape[0], BLOCK), lambda i, m: (0, i)),
                placed(conv_weight.shape[0]), placed(1),
            ],
            out_specs=[
                own, cube(8), cube(8),
                pl.BlockSpec((rows, LANES), whole),
                pl.BlockSpec((streams, 8, LANES), lambda i, m: (0, 0, 0)),
                pl.BlockSpec((rows, state_size), whole),
            ],
        ),
        out_shape=[
            jax.ShapeDtypeStruct(x.shape, LOW),
            jax.ShapeDtypeStruct((streams, 8, x.shape[1]), F32),
            jax.ShapeDtypeStruct((streams, 8, x.shape[1]), F32),
            jax.ShapeDtypeStruct((rows, LANES), F32),
            jax.ShapeDtypeStruct((streams, 8, LANES), F32),
            jax.ShapeDtypeStruct((rows, state_size), F32),
        ],
        compiler_params=pltpu.CompilerParams(vmem_limit_bytes=VMEM),
        name="after",
    )(meta, x, d_mixed, dxs, d_after, state, step, rest_d, b_low, skip, ci, conv_weight, conv_bias)


def finish_kernel(cfg, meta_ref, *refs):
    streams, length, slots, groups, per_group, headdim = cfg
    meta = Meta(meta_ref, groups, slots)
    dgts, dcs, dbs, directs, sums = (refs[i * groups : (i + 1) * groups] for i in range(5))
    row_sum, step, slope, through, rates, b_low, c_low, ci, cw, cb = refs[5 * groups : 5 * groups + 10]
    d_raw, dci, tail, spill = refs[5 * groups + 10 :]
    upper = (iota((length, length), 0) <= iota((length, length), 1)).astype(F32)
    add = lambda parts, at: functools.reduce(lambda a, b: a + b, [p[at] for p in parts])
    for s in range(streams):
        at = slice(s * length, (s + 1) * length)
        direct = add(directs, at)
        ends = add(sums, s)
        from_end = through[s, 0:1] * ends[0:1] + ends[1:2]
        d_log = dot(upper, row_sum[at] - step[at] * direct, HIGHEST) + from_end
        d_raw[at] = ((direct - rates[...] * d_log) * slope[at]).astype(LOW)
        seg_u = meta.segment(s, meta.first() + iota((length, length), 0))
        seg_t = meta.segment(s, meta.first() + iota((length, length), 1))
        dgt = jnp.where(seg_u == seg_t, upper, 0.0) * add(dgts, s)
        d_b = add(dbs, at) + dot(dgt.astype(LOW), c_low[at])
        d_c = add(dcs, at) + dot(jnp.transpose(dgt).astype(LOW), b_low[at])
        block = ci[s * (HALO + length) : (s + 1) * (HALO + length)].astype(F32)
        masks = tap_masks(meta, s, cw.shape[0], length)
        total = conv_back(jnp.concatenate([d_b, d_c], axis=1), block, masks, cw[...], cb[...])
        dci[at] = total[HALO:].astype(LOW)
        tail[s] = total[HALO + length - 8 :]
        spill[s] = total[HALO - 8 : HALO]


def finish(cfg, meta, dgts, dcs, dbs, directs, sums, row_sum, step, slope, through, rates, b_low, c_low, ci, conv_weight, conv_bias, block_at):
    streams, length, slots, groups, per_group, headdim = cfg
    rows = streams * length
    args = [*dgts, *dcs, *dbs, *directs, *sums, row_sum, step, slope, through, rates, b_low, c_low, ci]
    zeros = lambda n: (lambda i, m: (0,) * n)
    conv_at = lambda i, m: (0, block_at)
    outs = [
        jax.ShapeDtypeStruct((rows, LANES), LOW),
        jax.ShapeDtypeStruct((rows, BLOCK), LOW),
        jax.ShapeDtypeStruct((streams, 8, BLOCK), F32),
        jax.ShapeDtypeStruct((streams, 8, BLOCK), F32),
    ]
    return pl.pallas_call(
        functools.partial(finish_kernel, cfg),
        grid_spec=pltpu.PrefetchScalarGridSpec(
            num_scalar_prefetch=1, grid=(1,),
            in_specs=[pl.BlockSpec(a.shape, zeros(a.ndim)) for a in args]
            + [pl.BlockSpec((conv_weight.shape[0], BLOCK), conv_at), pl.BlockSpec((1, BLOCK), conv_at)],
            out_specs=[pl.BlockSpec(a.shape, zeros(len(a.shape))) for a in outs],
        ),
        out_shape=outs,
        compiler_params=pltpu.CompilerParams(vmem_limit_bytes=VMEM),
        name="finish",
    )(meta, *args, conv_weight, conv_bias)


def back_project_kernel(groups, blocks, shared, seeded, meta_ref, *refs):
    core = None
    ds, refs = (refs[:1] * groups, refs[1:]) if shared else (refs[:groups], refs[groups:])
    weights, refs = refs[: 2 * groups], refs[2 * groups :]
    hidden, up, refs = refs[0], refs[1], refs[2:]
    if seeded:
        dn_in, dh_in, refs = refs[0], refs[1], refs[2:]
    dn, dh, g_up = refs
    step = pl.program_id(0)

    @pl.when(step == 0)
    def _():
        dn[...] = dn_in[...] if seeded else jnp.zeros_like(dn)
        dh[...] = dh_in[...] if seeded else jnp.zeros_like(dh)

    for j in range(groups):

        @pl.when(lax.div(step, blocks) == j)
        def _():
            d = ds[j][...]
            dn[0] += dot_nt(d, weights[2 * j][...])
            dn[1] += dot_nt(d, weights[2 * j + 1][...])
            dh[...] += dot_nt(d, up[...])
            g_up[...] = jnp.transpose(
                lax.dot_general(hidden[...], d, (((0,), (0,)), ((), ())), preferred_element_type=F32)
            )


def back_project(cfg, meta, ds, weights, hidden, in_up, first_block, seed=None):
    streams, length, slots, groups, per_group, headdim = cfg
    shared = not isinstance(ds, list)
    rows = hidden.shape[0]
    cols = weights[0][0].shape[1]
    half = weights[-1][0].shape[0]
    blocks = cols // BLOCK
    core = core_at(groups, streams, slots)
    at = lambda i, m: m[lax.div(i, blocks)] * blocks + lax.rem(i, blocks)
    local_at = lambda i, j: jnp.clip(i - blocks * j, 0, blocks - 1)
    in_specs, args = [], []
    if shared:
        in_specs.append(pl.BlockSpec((rows, BLOCK), lambda i, m: (0, at(i, m))))
        args.append(ds)
    else:
        for j in range(groups):
            in_specs.append(pl.BlockSpec((rows, BLOCK), lambda i, m, j=j: (0, local_at(i, j))))
        args += ds
    for j, (mine, other) in enumerate(weights):
        same = mine is other
        in_specs.append(pl.BlockSpec((half, BLOCK), lambda i, m, j=j, s=same: (m[core] if s else 0, local_at(i, j))))
        in_specs.append(pl.BlockSpec((half, BLOCK), lambda i, m, j=j, s=same: (1 - m[core] if s else 0, local_at(i, j))))
        args += [mine, other]
    whole = lambda i, m: (0, 0)
    in_specs += [
        pl.BlockSpec(hidden.shape, whole),
        pl.BlockSpec((in_up.shape[0], BLOCK), lambda i, m: (0, first_block + at(i, m))),
    ]
    args += [hidden, in_up]
    dn_spec = pl.BlockSpec((2, rows, half), lambda i, m: (0, 0, 0))
    dh_spec = pl.BlockSpec((rows, in_up.shape[0]), whole)
    if seed is not None:
        in_specs += [dn_spec, dh_spec]
        args += list(seed)
    return pl.pallas_call(
        functools.partial(back_project_kernel, groups, blocks, shared, seed is not None),
        grid_spec=pltpu.PrefetchScalarGridSpec(
            num_scalar_prefetch=1, grid=(groups * blocks,), in_specs=in_specs,
            out_specs=[dn_spec, dh_spec, pl.BlockSpec((BLOCK, in_up.shape[0]), lambda i, m: (at(i, m), 0))],
        ),
        out_shape=[
            jax.ShapeDtypeStruct((2, rows, half), F32),
            jax.ShapeDtypeStruct((rows, in_up.shape[0]), F32),
            jax.ShapeDtypeStruct((groups * cols, in_up.shape[0]), F32),
        ],
        compiler_params=pltpu.CompilerParams(vmem_limit_bytes=VMEM),
        cost_estimate=pl.CostEstimate(
            flops=2 * rows * groups * cols * (2 * half + 512),
            bytes_accessed=groups * cols * (4 * half + 2 * rows) + 16 * rows * half,
            transcendentals=0,
        ),
        name="back_project",
    )(meta, *args)


def swap_cores(value):
    return lax.ppermute(value, "fsdp", [(i, i ^ 1) for i in range(lax.axis_size("fsdp"))])


def scan_states(own, kept_mine, kept_other, per_head, reverse):
    count = lax.axis_size("fsdp")
    core = lax.axis_index("fsdp") % 2
    half = own.shape[2] // 2
    mine = lax.dynamic_slice_in_dim(own, core * half, half, 2)
    other = swap_cores(lax.dynamic_slice_in_dim(own, (1 - core) * half, half, 2))
    early = (core == 1) if reverse else (core == 0)
    first = jnp.where(early, mine, other).astype(F32)
    second = jnp.where(early, other, mine).astype(F32)

    def spread(kept):
        kept = lax.dynamic_slice_in_dim(kept, core * (half // per_head), half // per_head, 1)
        return jnp.repeat(kept, per_head, axis=1)[:, None, :]

    kept_first = spread(jnp.where(early, kept_mine, kept_other))
    kept_second = spread(jnp.where(early, kept_other, kept_mine))
    added = kept_second * first + second
    kept_both = kept_first * kept_second
    entering = None
    for hop in range(count // 2 - 1):
        send = added if entering is None else kept_both * entering.astype(F32) + added
        chip = count // 2 - 1 - hop if reverse else hop
        route = [(2 * chip + c, 2 * (chip - 1 if reverse else chip + 1) + c) for c in (0, 1)]
        got = lax.ppermute(send.astype(LOW), "fsdp", route)
        entering = got if entering is None else entering + got
    entering = entering.astype(F32)
    entering_second = kept_first * entering + first
    keep = jnp.where(early, entering, entering_second).astype(LOW)
    got = swap_cores(jnp.where(early, entering_second, entering).astype(LOW))
    return jnp.where(core == 0, jnp.concatenate([keep, got], 2), jnp.concatenate([got, keep], 2))


def share_quarters(quarter):
    core = lax.axis_index("fsdp") % 2
    half = quarter.shape[0] // 2
    part = half // 2
    move = lambda v, bit: lax.ppermute(v, "dp", [(i, i ^ bit) for i in range(lax.axis_size("dp"))])
    mine = lax.dynamic_slice_in_dim(quarter, core * half, half, 0)
    one, two = move(mine, 1), move(mine, 2)
    both = jnp.concatenate([move(one[:part], 2), move(two[part:], 1)], axis=0)
    return [(quarter, quarter)] + [(v, swap_cores(v)) for v in (one, two, both)]


def rms_scale(values, gain_vec):
    mean_sq = jnp.mean(values * values, axis=-1, keepdims=True)
    return values * lax.rsqrt(mean_sq + EPSILON) * gain_vec


def local(
    block_input, seq_lengths, adapter_ids, norm_gain, w_in, w_dt, conv_weight, conv_bias, dt_bias,
    head_rates, skip_gain, gate_gain, w_out, in_down, in_up, out_down, out_up, out_grad,
):
    streams, length, width = block_input.shape[1:]
    inner = gate_gain.shape[0]
    taps, conv_cols = conv_weight.shape
    heads = dt_bias.shape[0]
    headdim = inner // heads
    state_size = (conv_cols - inner) // 2
    adapters, ranks = in_down.shape[:2]
    in_cols = in_up.shape[2]
    slots = seq_lengths.shape[2]
    rows = streams * length
    groups = lax.axis_size("dp")
    per_group = heads // groups
    group_cols = inner // groups
    cfg = (streams, length, slots, groups, per_group, headdim)
    count = lax.axis_size("fsdp")
    first_pos = lax.axis_index("fsdp") * length
    ends = jnp.cumsum(seq_lengths[0], axis=-1, dtype=jnp.int32)
    core = lax.axis_index("fsdp") % 2
    order = lax.axis_index("dp") ^ jnp.arange(groups, dtype=jnp.int32)
    meta = jnp.concatenate([order, first_pos[None], ends.reshape(-1), core[None]]).astype(jnp.int32)

    gather = lambda a: lax.all_gather(a, "fsdp", axis=0, tiled=True)
    quarter = lambda a: lax.dynamic_slice_in_dim(a, order[0] * group_cols, group_cols, 1)
    pad_heads = lambda a: jnp.pad(a, ((0, 0), (0, LANES - heads)))
    w_small = gather(jnp.concatenate([w_in[:, 2 * inner :], pad_heads(w_dt)], axis=1))
    w_bc, w_step = w_small[:, : 2 * state_size], w_small[:, 2 * state_size :]
    w_x = share_quarters(gather(quarter(w_in[:, inner : 2 * inner])))
    w_gate = share_quarters(gather(quarter(w_in[:, :inner])))
    w_o = gather(w_out)

    devices = range(count)
    before = lax.ppermute(block_input[0, :, length - HALO :], "fsdp", [(i - 1, i) for i in devices if i > 0])
    extended = jnp.concatenate([before, block_input[0]], axis=1)
    pos = first_pos - HALO + jnp.arange(length + HALO, dtype=jnp.int32)
    seg = jnp.sum((pos[None, :, None] >= ends[:, None, :]).astype(jnp.int32), axis=-1)
    seg = jnp.where(pos[None] < 0, -1, seg)
    slot_at = jnp.arange(slots, dtype=jnp.int32)
    member = (seg[:, :, None] == slot_at).astype(F32)
    chosen = (adapter_ids[0][:, :, None] == jnp.arange(adapters, dtype=jnp.int32)).astype(F32)
    onehot = jnp.einsum("slj,sjk->slk", member, chosen, precision=HIGHEST)
    allowed = jnp.repeat(onehot, ranks, axis=-1)
    allowed_ext = allowed.reshape(streams * (length + HALO), adapters * ranks)
    allowed = allowed[:, HALO:].reshape(rows, adapters * ranks)
    valid = (seg[:, HALO:] < slots).astype(F32).reshape(rows, 1)
    normed_ext = rms_scale(extended.reshape(-1, width).astype(F32), norm_gain).astype(LOW)
    down_in = in_down.reshape(adapters * ranks, width)
    up_in = in_up.reshape(adapters * ranks, in_cols)
    down_out = out_down.reshape(adapters * ranks, inner)
    up_out = out_up.reshape(adapters * ranks, width)
    hidden_ext = (dot_nt(normed_ext, down_in) * allowed_ext).astype(LOW)
    strip = lambda a: a.reshape(streams, length + HALO, -1)[:, HALO:].reshape(rows, -1)
    normed = strip(normed_ext)
    hidden_in = strip(hidden_ext)
    grad_rows = out_grad.reshape(rows, width).astype(F32)
    d_branch = (grad_rows * valid).astype(LOW)
    d_hidden_out = (dot_nt(d_branch, up_out) * allowed).astype(LOW)

    by_half = lambda a: jnp.stack([a[:, : width // 2], a[:, width // 2 :]])
    nx_ext, nx = by_half(normed_ext), by_half(normed)

    dt_in = dot(normed, w_step) + pad_heads(dt_bias[None])
    real = jnp.arange(LANES) < heads
    step = jnp.where(real, jax.nn.softplus(dt_in), 0.0)
    slope = jnp.where(real, jax.nn.sigmoid(dt_in), 0.0)
    rates = pad_heads(head_rates[None])
    bias_row = conv_bias[None]
    x_blocks = inner // BLOCK
    group_blocks = group_cols // BLOCK
    ci_bc, bc = project(cfg, meta, 0, nx_ext, hidden_ext, (w_bc, w_bc), up_in, conv_weight, bias_row, x_blocks, 1)
    (log_d, enter_d, rest_d, weight, log_t, through, g, gt, b_low, c_low, bt, ct) = decays(
        cfg, meta, step, rates, bc, heads
    )
    kept_mine = through[:, 0, :heads]
    kept_other = swap_cores(kept_mine)
    of_group = lambda a, j: lax.dynamic_slice_in_dim(a, order[j] * per_group, per_group, 1)

    ci, xs, states = [], [], []
    for j in range(groups):
        ci_j, x_j, own = project(
            cfg, meta, j, nx_ext, hidden_ext, w_x[j], up_in, conv_weight, bias_row, 0, group_blocks, weight, bt
        )
        ci.append(ci_j)
        xs.append(x_j)
        states.append(scan_states(own, of_group(kept_mine, j), of_group(kept_other, j), headdim, False))
    ys = [inside(cfg, meta, j, xs[j], step, log_d, log_t, g) for j in range(groups)]
    gates = [gate_project(cfg, meta, j, nx, hidden_in, w_gate[j], up_in) for j in range(groups)]
    d_normed_out = dot_nt(d_branch, w_o) + dot(d_hidden_out, down_out)

    skip_row = jnp.repeat(skip_gain, headdim)[None]
    out_low, d_mixed, d_gate, row_sum, d_state = gated(
        cfg, meta, xs, ys, states, gates, d_normed_out, enter_d, c_low, ct, skip_row, gate_gain[None]
    )
    d_state = d_state.astype(LOW)
    afters = []
    for j in range(groups):
        part = lax.dynamic_slice_in_dim(d_state, order[j] * group_cols, group_cols, 2)
        afters.append(scan_states(part, of_group(kept_mine, j), of_group(kept_other, j), headdim, True))

    hidden_out = (dot_nt(out_low, down_out) * allowed).astype(LOW)
    branch = (dot(out_low, w_o) + dot(hidden_out, up_out)) * valid
    block_output = (block_input.reshape(rows, width).astype(F32) + branch).astype(LOW)
    turn = lambda a, b: lax.dot_general(a, b, (((0,), (0,)), ((), ())), preferred_element_type=F32)
    g_out_up = turn(d_branch, hidden_out)
    g_out_down = turn(out_low, d_hidden_out)

    dxs, dgts, dcs = [], [], []
    for j in range(groups):
        a, b, c = inside_back(cfg, meta, j, xs[j], d_mixed, step, log_d, enter_d, log_t, gt, states[j])
        dxs.append(a)
        dgts.append(b)
        dcs.append(c)
    dcis, tails, spills, directs, sums, dbs = [], [], [], [], [], []
    for j in range(groups):
        got = after(
            cfg, meta, j, xs[j], d_mixed, dxs[j], afters[j], states[j], step, rest_d, b_low, skip_row,
            ci[j], conv_weight, bias_row,
        )
        for into, what in zip((dcis, tails, spills, directs, sums, dbs), got):
            into.append(what)
    d_raw, dci_bc, tail_bc, spill_bc = finish(
        cfg, meta, dgts, dcs, dbs, directs, sums, row_sum, step, slope, through, rates, b_low, c_low,
        ci_bc, conv_weight, bias_row, x_blocks,
    )
    spilled = lax.ppermute(
        jnp.concatenate(spills + [spill_bc], axis=2), "fsdp", [(i, i - 1) for i in devices if i > 0]
    )
    tail = (jnp.concatenate(tails + [tail_bc], axis=2) + spilled).astype(LOW)
    d_parts = []
    for j, part in enumerate(dcis + [dci_bc]):
        part = part.reshape(streams, length, -1)
        end = tail[:, :, j * group_cols : j * group_cols + part.shape[2]]
        d_parts.append(lax.dynamic_update_slice(part, end, (0, length - 8, 0)).reshape(rows, -1))
    d_bc = d_parts.pop()

    gate_blocks = inner // BLOCK
    early = back_project(cfg, meta, d_gate, w_gate, hidden_in, up_in, 0)
    late = back_project(cfg, meta, d_parts, w_x, hidden_in, up_in, gate_blocks, early[:2])
    up_bc = up_in[:, 2 * inner :]
    d_hidden_in = ((late[1] + dot_nt(d_bc, up_bc)) * allowed).astype(LOW)
    back = late[0]
    back = jnp.where(core == 0, jnp.concatenate([back[0], back[1]], 1), jnp.concatenate([back[1], back[0]], 1))
    d_normed = back + dot_nt(d_bc, w_bc) + dot_nt(d_raw, w_step) + dot(d_hidden_in, down_in)
    inputs = block_input.reshape(rows, width).astype(F32)
    rs = lax.rsqrt(jnp.mean(inputs * inputs, axis=-1, keepdims=True) + EPSILON)
    scaled = d_normed * norm_gain
    cross = jnp.mean(scaled * inputs, axis=-1, keepdims=True)
    input_grad = grad_rows + rs * (scaled - inputs * (rs * rs * cross))
    g_in_up = jnp.concatenate([early[2], late[2], turn(d_bc, hidden_in)], axis=0)
    g_in_down = turn(normed, d_hidden_in)
    totals = [
        lax.psum(lax.psum_scatter(a, "fsdp", scatter_dimension=0, tiled=True), "dp").T.reshape(adapters, ranks, -1)
        for a in (g_in_down, g_in_up, g_out_down, g_out_up)
    ]
    return (block_output.reshape(1, streams, length, width), input_grad.reshape(1, streams, length, width), *totals)


def solution(mesh):
    rows = P("dp", None, "fsdp", None)
    cut = P("fsdp", None)
    per_group = P("dp", None, None)
    in_specs = (
        rows, per_group, per_group, P(), cut, cut, P(), P(), P(), P(), P(), P(), cut, P(), P(), P(), P(), rows,
    )
    out_specs = (rows, rows) + (P(None, None, "fsdp"),) * 4
    return jax.shard_map(local, mesh=mesh, in_specs=in_specs, out_specs=out_specs, check_vma=False)
```

time: 1190 us -> 698 us (0.59)
  waiting for transfers between devices: 583 us -> 200 us
  matrix products: 273 us -> 40.4 us
  Pallas kernels: 0 us -> 201 us
  other arithmetic: 131 us -> 42.6 us
  starting transfers between devices: 4.09 us -> 58 us
  local copies, waits for them, and re-layouts: 150 us -> 121 us
  blocking collectives: 28.7 us -> 0 us
    all_gather x4, waiting for transfers between devices: 536 us -> 10.8 us  [local(): gather = lambda a: lax.all_gather(a, 'fsdp', axis=0, tiled=True)]
    dot_general x31 -> x17, matrix products: 273 us -> 40.4 us  [the longest x5 19.4 us: dot(): lax.dot_general(a, b, (((1,), (0,)), ((), ())), precision=precision, pref...]
    pallas_call x0 -> x26, Pallas kernels: none -> 201 us  [the longest x4 37.1 us: after(): pl.pallas_call(functools.partial(after_kernel, cfg, slot), grid_spec=pltp...]
    reduce_scatter x1 -> x4, waiting for transfers between devices: 0.01 us -> 75.3 us  [local(): lax.psum_scatter(a, 'fsdp', scatter_dimension=0, tiled=True)]
    ppermute x2 -> x57, waiting for transfers between devices: 0.42 us -> 65.2 us  [the longest x8 33 us: share_quarters(): lax.ppermute(v, 'dp', [(i, i ^ bit) for i in range(lax.axis_size('dp'))])]
    ppermute x2 -> x57, starting transfers between devices: 3.72 us -> 57.3 us  [the longest x24 36.3 us: scan_states(): got = lax.ppermute(send.astype(LOW), 'fsdp', route)]
    unnamed x194 -> x360, local copies, waits for them, and re-layouts: 82.9 us -> 37.5 us
    add x9 -> x2, other arithmetic: 39.1 us -> 4.81 us  [the longest x1 4.81 us: local(): input_grad = grad_rows + rs * (scaled - inputs * (rs * rs * cross))]
  transfers between devices with their start and end apart: 11 -> 66, of which waited for: 6 -> 14; matrix products, arithmetic and copies ran while one was open for 35% -> 22% of each run, Pallas kernels for 0% -> 26%
where the time goes in v1:
time: 698 us; the launch traced here: 685 us
  Pallas kernels  201 us (29%)
  waiting for transfers between devices  200 us (29%)
  local copies, waits for them, and re-layouts  121 us (17%)
  starting transfers between devices  58 us (8%)
  other arithmetic  42.6 us (6%)
  matrix products  40.4 us (6%)
  between operations  22.3 us (3%)
    reduce_scatter x4, waiting for transfers between devices, local(): lax.psum_scatter(a, 'fsdp', scatter_dimension=0, tiled=True)  75.3 us
    psum x1, waiting for transfers between devices, local(): lax.psum(lax.psum_scatter(a, 'fsdp', scatter_dimension=0, tiled=True), 'dp')  47.6 us
    unnamed x360, local copies, waits for them, and re-layouts  37.5 us
    pallas_call x4, Pallas kernels, after(): pl.pallas_call(functools.partial(after_kernel, cfg, slot), grid_spec=pltp...  37.1 us
    ppermute x24, starting transfers between devices, scan_states(): got = lax.ppermute(send.astype(LOW), 'fsdp', route)  36.3 us
    pallas_call x5, Pallas kernels, project(): pl.pallas_call(functools.partial(project_kernel, cfg, slot, with_state),...  35.3 us
    pallas_call x2, Pallas kernels, back_project(): pl.pallas_call(functools.partial(back_project_kernel, groups, blocks, sha...  34.2 us
    ppermute x8, waiting for transfers between devices, share_quarters(): lax.ppermute(v, 'dp', [(i, i ^ bit) for i in range(lax.axis_size('dp'))])  33 us
  transfers between devices with their start and end apart: 66, of which 14 were waited for; matrix products, arithmetic and copies ran while one was open for 22% of the time, Pallas kernels for 26%

profile of v1, /device:TPU:0, one launch (start us, length us, event | category | flops | bytes accessed | tf_op | source)
XLA Modules:
  0.0 685.0 jit_solution(3927038259553358030)
XLA Ops:
  11.1 2.8 fusion.61
  17.7 2.3 collective-permute-start
  43.5 2.5 divide_select_fusion
  54.4 2.6 collective-permute-start.8
  58.5 10.8 %all-gather.5.cloned.1.call-done.w_mine.w_other.refs_4_.refs_5_ = bf16[1536,768]{1,0:T(8,128)(2,1)} async-done(((bf16[192,768]{1,0:T(8,128)(2,1)}), bf16[1536,768]{1,0:T(8,128)(2,1)}) %all-gather.5.cloned.1.call-update) | async-done | bytes 2359312 | tf_op jit(solution)/shard_map/all_gather | solution.py:855
  72.7 8.3 %project_conv.6 = (bf16[544,768]{1,0:T(8,128)(2,1)S(1)}, f32[512,768]{1,0:T(8,128)S(1)}, bf16[2,128,768]{2,1,0:T(8,128)(2,1)S(1)}) custom-call(s32[12]{0:T(128)S(1)} %pad_add_fusion.meta_ref, bf16[2,544,768]{2,1,0:T(8,128)(2,1)} %pad_maximum_fusion.1.nx, bf16[544,128]{1,0:T(8,128)(2,1)S(1)} %fusion.11.hx, ...), custom_call_target="tpu_custom_call" | custom-call | flops 1497366528 | bytes 5701632 | tf_op jit(solution)/shard_map/project_conv/pallas_call | solution.py:238
  94.9 3.6 collective-permute-start.10
  113.8 16.2 %collective-permute-done.1.w_mine.refs_6_ = bf16[768,768]{1,0:T(8,128)(2,1)} collective-permute-done((bf16[768,768]{1,0:T(8,128)(2,1)}, bf16[768,768]{1,0:T(8,128)(2,1)}, u32[]{:S(2)}, u32[]{:S(2)}) %collective-permute-start.1) | collective-permute-done | bytes 1179680 | tf_op jit(solution)/shard_map/ppermute | solution.py:818
  138.4 16.8 %collective-permute-done.29.w_mine.refs_3_ = bf16[768,768]{1,0:T(8,128)(2,1)S(1)} collective-permute-done((bf16[768,768]{1,0:T(8,128)(2,1)S(1)}, bf16[768,768]{1,0:T(8,128)(2,1)S(1)}, u32[]{:S(2)}, u32[]{:S(2)}) %collective-permute-start.29) | collective-permute-done | bytes 1179680 | tf_op jit(solution)/shard_map/ppermute | solution.py:818
  209.7 4.2 project_gate.4.refs_12_
  214.0 5.0 inside.4.refs_4_
  224.6 8.4 %project_conv.8 = (bf16[544,768]{1,0:T(8,128)(2,1)S(1)}, f32[512,768]{1,0:T(8,128)S(1)}, bf16[2,128,768]{2,1,0:T(8,128)(2,1)S(1)}) custom-call(s32[12]{0:T(128)S(1)} %pad_add_fusion.meta_ref, bf16[2,544,768]{2,1,0:T(8,128)(2,1)} %pad_maximum_fusion.1.nx, bf16[544,128]{1,0:T(8,128)(2,1)S(1)} %fusion.11.hx, ...), custom_call_target="tpu_custom_call" | custom-call | flops 1497366528 | bytes 5701632 | tf_op jit(solution)/shard_map/project_conv/pallas_call | solution.py:238
  233.0 5.0 inside.6.refs_6_
  238.4 8.5 %project_conv.7 = (bf16[544,768]{1,0:T(8,128)(2,1)S(1)}, f32[512,768]{1,0:T(8,128)S(1)}, bf16[2,128,768]{2,1,0:T(8,128)(2,1)S(1)}) custom-call(s32[12]{0:T(128)S(1)} %pad_add_fusion.meta_ref, bf16[2,544,768]{2,1,0:T(8,128)(2,1)} %pad_maximum_fusion.1.nx, bf16[544,128]{1,0:T(8,128)(2,1)S(1)} %fusion.11.hx, ...), custom_call_target="tpu_custom_call" | custom-call | flops 1497366528 | bytes 5701632 | tf_op jit(solution)/shard_map/project_conv/pallas_call | solution.py:238
  248.3 4.0 project_gate.5.refs_13_
  252.2 5.0 inside.5.refs_5_
  257.3 4.1 project_gate.6.refs_14_
  263.0 12.6 %collective-permute-start.15 = (bf16[2,128,384]{2,1,0:T(8,128)(2,1)S(1)}, bf16[2,128,384]{2,1,0:T(8,128)(2,1)S(1)}, u32[]{:S(2)}, u32[]{:S(2)}) collective-permute-start(bf16[2,128,384]{2,1,0:T(8,128)(2,1)S(1)} %get-tuple-element.196), channel_id=1, source_target_pairs={{0,2},{1,3},{8,10},{9,11},{16,18},{17,19},{24,26},{25,27}} | collective-permute-start | bytes 589832 | tf_op jit(solution)/shard_map/ppermute | solution.py:805
  277.3 8.2 %project_conv.9 = (bf16[544,768]{1,0:T(8,128)(2,1)S(1)}, f32[512,768]{1,0:T(8,128)S(1)}, bf16[2,128,768]{2,1,0:T(8,128)(2,1)S(1)}) custom-call(s32[12]{0:T(128)S(1)} %pad_add_fusion.meta_ref, bf16[2,544,768]{2,1,0:T(8,128)(2,1)} %pad_maximum_fusion.1.nx, bf16[544,128]{1,0:T(8,128)(2,1)S(1)} %fusion.11.hx, ...), custom_call_target="tpu_custom_call" | custom-call | flops 1497366528 | bytes 5701632 | tf_op jit(solution)/shard_map/project_conv/pallas_call | solution.py:238
  289.8 5.0 inside.7.refs_7_
  294.9 4.0 project_gate.7.refs_15_
  303.2 8.2 %fusion.63 = f32[512,3072]{1,0:T(8,128)S(1)} fusion(bf16[512,1536]{1,0:T(8,128)(2,1)} %fusion.6, bf16[3072,1536]{1,0:T(8,128)(2,1)} %all-gather.11.cloned.1.call-done), kind=kOutput, calls=%fused_computation.264 | convolution fusion | flops 4831838208 | bytes 17301504 | tf_op jit(solution)/shard_map/dot_general | solution.py:26
  311.5 3.6 convolution_add_fusion.refs_16_
  315.2 26.3 %gated.1 = (bf16[512,3072]{1,0:T(8,128)(2,1)}, f32[512,3072]{1,0:T(8,128)}, bf16[512,3072]{1,0:T(8,128)(2,1)}, f32[512,128]{1,0:T(8,128)S(1)}, f32[2,128,3072]{2,1,0:T(8,128)}) custom-call(s32[12]{0:T(128)S(1)} %pad_add_fusion.meta_ref, f32[512,768]{1,0:T(8,128)} %copy-done.6, f32[512,768]{1,0:T(8,128)} %copy-done.13, f32[512,768]{1,0:T(8,128)} %copy-done.9, ...), custom_call_target="tpu_custom_call" | custom-call | tf_op jit(solution)/shard_map/gated/pallas_call | solution.py:453
  351.3 16.5 %back_project.2 = (f32[2,512,768]{2,1,0:T(8,128)}, f32[512,128]{1,0:T(8,128)S(1)}, f32[3072,128]{1,0:T(8,128)}) custom-call(s32[12]{0:T(128)S(1)} %pad_add_fusion.meta_ref, bf16[512,3072]{1,0:T(8,128)(2,1)} %get-tuple-element.151.refs_0_, bf16[1536,768]{1,0:T(8,128)(2,1)} %all-gather.9.cloned.1.call-done.w_mine.w_other.refs_1_.refs_2_, ...), custom_call_target="tpu_custom_call" | custom-call | flops 6442450944 | bytes 18874368 | tf_op jit(solution)/shard_map/back_project/pallas_call | solution.py:757
  367.8 6.7 inside_back.5
  375.7 6.8 inside_back.4
  383.7 3.1 fusion.40
  387.5 6.7 inside_back.6
  395.5 6.7 inside_back.7
  413.8 18.2 %collective-permute-done.44 = bf16[2,128,384]{2,1,0:T(8,128)(2,1)S(1)} collective-permute-done((bf16[2,128,384]{2,1,0:T(8,128)(2,1)S(1)}, bf16[2,128,384]{2,1,0:T(8,128)(2,1)S(1)}, u32[]{:S(2)}, u32[]{:S(2)}) %collective-permute-start.44) | collective-permute-done | bytes 196640 | tf_op jit(solution)/shard_map/ppermute | solution.py:805
  432.2 4.3 collective-permute-done.39
  436.7 3.1 collective-permute-done.49
  440.0 3.5 collective-permute-done.54
  443.9 9.2 %after.5 = (bf16[512,768]{1,0:T(8,128)(2,1)S(1)}, f32[2,8,768]{2,1,0:T(8,128)S(1)}, f32[2,8,768]{2,1,0:T(8,128)S(1)}, f32[512,128]{1,0:T(8,128)S(1)}, f32[2,8,128]{2,1,0:T(8,128)S(1)}, /*index=5*/f32[512,128]{1,0:T(8,128)S(1)}) custom-call(s32[12]{0:T(128)S(1)} %pad_add_fusion.meta_ref, f32[512,768]{1,0:T(8,128)S(1)} %copy-done.14, ...), custom_call_target="tpu_custom_call" | custom-call | tf_op jit(solution)/shard_map/after/pallas_call | solution.py:611
  453.2 9.2 %after.4 = (bf16[512,768]{1,0:T(8,128)(2,1)S(1)}, f32[2,8,768]{2,1,0:T(8,128)S(1)}, f32[2,8,768]{2,1,0:T(8,128)S(1)}, f32[512,128]{1,0:T(8,128)S(1)}, f32[2,8,128]{2,1,0:T(8,128)S(1)}, /*index=5*/f32[512,128]{1,0:T(8,128)S(1)}) custom-call(s32[12]{0:T(128)S(1)} %pad_add_fusion.meta_ref, f32[512,768]{1,0:T(8,128)S(1)} %copy-done.8, ...), custom_call_target="tpu_custom_call" | custom-call | tf_op jit(solution)/shard_map/after/pallas_call | solution.py:611
  462.6 9.2 %after.6 = (bf16[512,768]{1,0:T(8,128)(2,1)S(1)}, f32[2,8,768]{2,1,0:T(8,128)S(1)}, f32[2,8,768]{2,1,0:T(8,128)S(1)}, f32[512,128]{1,0:T(8,128)S(1)}, f32[2,8,128]{2,1,0:T(8,128)S(1)}, /*index=5*/f32[512,128]{1,0:T(8,128)S(1)}) custom-call(s32[12]{0:T(128)S(1)} %pad_add_fusion.meta_ref, f32[512,768]{1,0:T(8,128)S(1)} %copy-done.10, ...), custom_call_target="tpu_custom_call" | custom-call | tf_op jit(solution)/shard_map/after/pallas_call | solution.py:611
  472.0 9.4 %after.7 = (bf16[512,768]{1,0:T(8,128)(2,1)S(1)}, f32[2,8,768]{2,1,0:T(8,128)S(1)}, f32[2,8,768]{2,1,0:T(8,128)S(1)}, f32[512,128]{1,0:T(8,128)S(1)}, f32[2,8,128]{2,1,0:T(8,128)S(1)}, /*index=5*/f32[512,128]{1,0:T(8,128)S(1)}) custom-call(s32[12]{0:T(128)S(1)} %pad_add_fusion.meta_ref, f32[512,768]{1,0:T(8,128)S(1)} %copy-done.12, ...), custom_call_target="tpu_custom_call" | custom-call | tf_op jit(solution)/shard_map/after/pallas_call | solution.py:611
  481.5 3.8 finish.1
  489.8 17.7 %back_project.3 = (f32[2,512,768]{2,1,0:T(8,128)}, f32[512,128]{1,0:T(8,128)S(1)}, f32[3072,128]{1,0:T(8,128)}) custom-call(s32[12]{0:T(128)S(1)} %pad_add_fusion.meta_ref, bf16[512,768]{1,0:T(8,128)(2,1)S(1)} %bitcast.160, bf16[512,768]{1,0:T(8,128)(2,1)S(1)} %bitcast.158, bf16[512,768]{1,0:T(8,128)(2,1)S(1)} %bitcast.162, bf16[512,768]{1,0:T(8,128)(2,1)S(1)} %bitcast.164, ...), custom_call_target="tpu_custom_call" | custom-call | flops 6442450944 | bytes 18874368 | tf_op jit(solution)/shard_map/back_project/pallas_call | solution.py:757
  509.3 4.1 fusion.66
  514.8 3.3 pad_maximum_fusion
  521.8 10.3 %fusion.10 = bf16[512,1536]{1,0:T(8,128)(2,1)} fusion(f32[512,1536]{1,0:T(8,128)S(1)} %fusion.64, bf16[512,3072]{1,0:T(8,128)(2,1)S(1)} %copy-done.91, bf16[3072,1536]{1,0:T(8,128)(2,1)} %all-gather.11.cloned.1.call-done, f32[512]{0:T(512)S(1)} %bitcast.193, bf16[512,1536]{1,0:T(8,128)(2,1)S(1)} %bitcast.168), kind=kOutput, calls=%fused_computation.26 | convolution fusion | flops 4835770368 | bytes 18876416 | tf_op jit(solution)/shard_map/dot_general | solution.py:20
  535.1 2.4 fusion.7
  543.1 33.0 %reduce-scatter.9.cloned.1.call-done = f32[384,128]{1,0:T(8,128)} async-done(((f32[3072,128]{1,0:T(8,128)}), f32[384,128]{1,0:T(8,128)}) %reduce-scatter.9.cloned.1.call-update) | async-done | bytes 196624 | tf_op jit(solution)/shard_map/reduce_scatter | solution.py:984
  577.9 40.0 %reduce-scatter.7.cloned.1.call-done = f32[800,128]{1,0:T(8,128)} async-done(((f32[6400,128]{1,0:T(8,128)}), f32[800,128]{1,0:T(8,128)}) %reduce-scatter.7.cloned.1.call-update) | async-done | bytes 409616 | tf_op jit(solution)/shard_map/reduce_scatter | solution.py:984
  619.9 4.8 bitcast_add_fusion
  624.7 47.6 %all-reduce.6.cloned.1.call-done = (f32[8,16,192]{2,1,0:T(8,128)}, f32[8,16,800]{2,1,0:T(8,128)}, f32[8,16,384]{2,1,0:T(8,128)}, f32[8,16,192]{2,1,0:T(8,128)}) async-done(((f32[8,16,192]{2,1,0:T(8,128)}, f32[8,16,800]{2,1,0:T(8,128)}, f32[8,16,384]{2,1,0:T(8,128)}, f32[8,16,192]{2,1,0:T(8,128)}), (f32[8,16,192]{2,1,0:T(8,128)}, f32[8,16,800]{2,1,0:T(8,128)}, f32[8,16,384]{2,1,0:T(8,128)}, ...) | async-done | bytes 802832 | tf_op jit(solution)/shard_map/psum | solution.py:984
  (658 shorter events, 205.1 us)
Async XLA Ops:
  7.2 31.6 %all-gather.7.cloned.1.call-start = ((), (), s32[]{:S(2)}) async-start(), calls=%async_computation.5 | async-start | bytes 1327104 | tf_op jit(solution)/shard_map/all_gather | solution.py:855
  9.8 59.6 %all-gather.5.cloned.1.call-start = ((), (), s32[]{:S(2)}) async-start(), calls=%async_computation.4 | async-start | bytes 2654208 | tf_op jit(solution)/shard_map/all_gather | solution.py:855
  14.6 89.2 %all-gather.9.cloned.1.call-start = ((), (), s32[]{:S(2)}) async-start(), calls=%async_computation.6 | async-start | bytes 2654208 | tf_op jit(solution)/shard_map/all_gather | solution.py:855
  16.4 286.8 %all-gather.11.cloned.1.call-start = ((), (), s32[]{:S(2)}) async-start(), calls=%async_computation.7 | async-start | bytes 10616832 | tf_op jit(solution)/shard_map/all_gather | solution.py:855
  17.0 520.5 %reduce-scatter.11.cloned.1.call-start = ((), (), s32[]{:S(2)}) async-start(), calls=%async_computation.11 | async-start | bytes 884736 | tf_op jit(solution)/shard_map/reduce_scatter | solution.py:984
  17.7 16.0 %collective-permute-start = (bf16[2,16,1536]{2,1,0:T(8,128)(2,1)}, bf16[2,16,1536]{2,1,0:T(8,128)(2,1)S(1)}, u32[]{:S(2)}, u32[]{:S(2)}) collective-permute-start(bf16[2,16,1536]{2,1,0:T(8,128)(2,1)} %slice_bitcast_fusion.6), channel_id=1, source_target_pairs={{0,1},{1,2},{2,3},{3,4},{4,5},{5,6},{6,7},{8,9},{9,10},{10,11},{11... | collective-permute-start | bytes 294920 | tf_op jit(solution)/shard_map/ppermute | solution.py:865
  54.4 30.4 %collective-permute-start.8 = (f32[2,48]{1,0:T(2,128)}, f32[2,48]{1,0:T(2,128)}, u32[]{:S(2)}, u32[]{:S(2)}) collective-permute-start(f32[2,48]{1,0:T(2,128)} %bitcast.18), channel_id=1, source_target_pairs={{0,1},{1,0},{2,3},{3,2},{4,5},{5,4},{6,7},{7,6},{8,9},{9,8},{10,11... | collective-permute-start | bytes 1160 | tf_op jit(solution)/shard_map/ppermute | solution.py:779
  94.9 11.0 %collective-permute-start.10 = (bf16[2,128,384]{2,1,0:T(8,128)(2,1)}, bf16[2,128,384]{2,1,0:T(8,128)(2,1)}, u32[]{:S(2)}, u32[]{:S(2)}) collective-permute-start(bf16[2,128,384]{2,1,0:T(8,128)(2,1)} %get-tuple-element.201), channel_id=1, source_target_pairs={{0,2},{1,3},{8,10},{9,11},{16,18},{17,19},{24,26},{25,27}} | collective-permute-start | bytes 589832 | tf_op jit(solution)/shard_map/ppermute | solution.py:805
  100.9 29.2 %collective-permute-start.1 = (bf16[768,768]{1,0:T(8,128)(2,1)}, bf16[768,768]{1,0:T(8,128)(2,1)}, u32[]{:S(2)}, u32[]{:S(2)}) collective-permute-start(bf16[768,768]{1,0:T(8,128)(2,1)} %constant_dynamic-slice_fusion.34), channel_id=1, source_target_pairs={{0,8},{8,0},{16,24},{24,16},{1,9},{9,1},{17,25},{25,17},{2,10},{10... | collective-permute-start | bytes 3538952 | tf_op jit(solution)/shard_map/ppermute | solution.py:818
  102.3 32.6 %collective-permute-start.3 = (bf16[768,768]{1,0:T(8,128)(2,1)}, bf16[768,768]{1,0:T(8,128)(2,1)}, u32[]{:S(2)}, u32[]{:S(2)}) collective-permute-start(bf16[768,768]{1,0:T(8,128)(2,1)} %constant_dynamic-slice_fusion.34), channel_id=1, source_target_pairs={{0,16},{8,24},{16,0},{24,8},{1,17},{9,25},{17,1},{25,9},{2,18},{10... | collective-permute-start | bytes 3538952 | tf_op jit(solution)/shard_map/ppermute | solution.py:818
  105.3 49.9 %collective-permute-start.29 = (bf16[768,768]{1,0:T(8,128)(2,1)S(1)}, bf16[768,768]{1,0:T(8,128)(2,1)S(1)}, u32[]{:S(2)}, u32[]{:S(2)}) collective-permute-start(bf16[768,768]{1,0:T(8,128)(2,1)S(1)} %constant_dynamic-slice_fusion.12), channel_id=1, source_target_pairs={{0,8},{8,0},{16,24},{24,16},{1,9},{9,1},{17,25},{25,17},{2,10},{10... | collective-permute-start | bytes 3538952 | tf_op jit(solution)/shard_map/ppermute | solution.py:818
  107.8 52.1 %collective-permute-start.31 = (bf16[768,768]{1,0:T(8,128)(2,1)S(1)}, bf16[768,768]{1,0:T(8,128)(2,1)}, u32[]{:S(2)}, u32[]{:S(2)}) collective-permute-start(bf16[768,768]{1,0:T(8,128)(2,1)S(1)} %constant_dynamic-slice_fusion.12), channel_id=1, source_target_pairs={{0,16},{8,24},{16,0},{24,8},{1,17},{9,25},{17,1},{25,9},{2,18},{10... | collective-permute-start | bytes 3538952 | tf_op jit(solution)/shard_map/ppermute | solution.py:818
  111.5 21.9 %collective-permute-start.12 = (bf16[2,128,384]{2,1,0:T(8,128)(2,1)S(1)}, bf16[2,128,384]{2,1,0:T(8,128)(2,1)S(1)}, u32[]{:S(2)}, u32[]{:S(2)}) collective-permute-start(bf16[2,128,384]{2,1,0:T(8,128)(2,1)S(1)} %get-tuple-element.199), channel_id=1, source_target_pairs={{4,6},{5,7},{12,14},{13,15},{20,22},{21,23},{28,30},{29,31}} | collective-permute-start | bytes 589832 | tf_op jit(solution)/shard_map/ppermute | solution.py:805
  131.9 73.9 %collective-permute-start.5 = (bf16[384,768]{1,0:T(8,128)(2,1)}, bf16[384,768]{1,0:T(8,128)(2,1)}, u32[]{:S(2)}, u32[]{:S(2)}) collective-permute-start(bf16[384,768]{1,0:T(8,128)(2,1)} %slice.149), channel_id=1, source_target_pairs={{0,16},{8,24},{16,0},{24,8},{1,17},{9,25},{17,1},{25,9},{2,18},{10... | collective-permute-start | bytes 1769480 | tf_op jit(solution)/shard_map/ppermute | solution.py:818
  134.3 22.8 %collective-permute-start.13 = (bf16[2,128,384]{2,1,0:T(8,128)(2,1)S(1)}, bf16[2,128,384]{2,1,0:T(8,128)(2,1)S(1)}, u32[]{:S(2)}, u32[]{:S(2)}) collective-permute-start(bf16[2,128,384]{2,1,0:T(8,128)(2,1)S(1)} %get-tuple-element.240), channel_id=1, source_target_pairs={{0,1},{1,0},{2,3},{3,2},{4,5},{5,4},{6,7},{7,6},{8,9},{9,8},{10,11... | collective-permute-start | bytes 589832 | tf_op jit(solution)/shard_map/ppermute | solution.py:779
  136.9 82.0 %collective-permute-start.6 = (bf16[384,768]{1,0:T(8,128)(2,1)}, bf16[384,768]{1,0:T(8,128)(2,1)}, u32[]{:S(2)}, u32[]{:S(2)}) collective-permute-start(bf16[384,768]{1,0:T(8,128)(2,1)} %slice.150), channel_id=1, source_target_pairs={{0,8},{8,0},{16,24},{24,16},{1,9},{9,1},{17,25},{25,17},{2,10},{10... | collective-permute-start | bytes 1769480 | tf_op jit(solution)/shard_map/ppermute | solution.py:818
  155.2 69.1 %collective-permute-start.4 = (bf16[768,768]{1,0:T(8,128)(2,1)}, bf16[768,768]{1,0:T(8,128)(2,1)}, u32[]{:S(2)}, u32[]{:S(2)}) collective-permute-start(bf16[768,768]{1,0:T(8,128)(2,1)} %collective-permute-done.3.w_mine.refs_8_), channel_id=1, source_target_pairs={{0,1},{1,0},{2,3},{3,2},{4,5},{5,4},{6,7},{7,6},{8,9},{9,8},{10,11... | collective-permute-start | bytes 3538952 | tf_op jit(solution)/shard_map/ppermute | solution.py:779
  157.1 63.1 %collective-permute-start.33 = (bf16[384,768]{1,0:T(8,128)(2,1)}, bf16[384,768]{1,0:T(8,128)(2,1)}, u32[]{:S(2)}, u32[]{:S(2)}) collective-permute-start(bf16[384,768]{1,0:T(8,128)(2,1)} %slice.154), channel_id=1, source_target_pairs={{0,16},{8,24},{16,0},{24,8},{1,17},{9,25},{17,1},{25,9},{2,18},{10... | collective-permute-start | bytes 1769480 | tf_op jit(solution)/shard_map/ppermute | solution.py:818
  159.9 78.2 %collective-permute-start.2 = (bf16[768,768]{1,0:T(8,128)(2,1)}, bf16[768,768]{1,0:T(8,128)(2,1)}, u32[]{:S(2)}, u32[]{:S(2)}) collective-permute-start(bf16[768,768]{1,0:T(8,128)(2,1)} %collective-permute-done.1.w_mine.refs_6_), channel_id=1, source_target_pairs={{0,1},{1,0},{2,3},{3,2},{4,5},{5,4},{6,7},{7,6},{8,9},{9,8},{10,11... | collective-permute-start | bytes 3538952 | tf_op jit(solution)/shard_map/ppermute | solution.py:779
  205.8 18.0 %collective-permute-start.34 = (bf16[384,768]{1,0:T(8,128)(2,1)S(1)}, bf16[384,768]{1,0:T(8,128)(2,1)S(1)}, u32[]{:S(2)}, u32[]{:S(2)}) collective-permute-start(bf16[384,768]{1,0:T(8,128)(2,1)S(1)} %slice.155), channel_id=1, source_target_pairs={{0,8},{8,0},{16,24},{24,16},{1,9},{9,1},{17,25},{25,17},{2,10},{10... | collective-permute-start | bytes 1769480 | tf_op jit(solution)/shard_map/ppermute | solution.py:818
  219.0 28.9 %collective-permute-start.30 = (bf16[768,768]{1,0:T(8,128)(2,1)S(1)}, bf16[768,768]{1,0:T(8,128)(2,1)}, u32[]{:S(2)}, u32[]{:S(2)}) collective-permute-start(bf16[768,768]{1,0:T(8,128)(2,1)S(1)} %copy-done.46), channel_id=1, source_target_pairs={{0,1},{1,0},{2,3},{3,2},{4,5},{5,4},{6,7},{7,6},{8,9},{9,8},{10,11... | collective-permute-start | bytes 3538952 | tf_op jit(solution)/shard_map/ppermute | solution.py:779
  220.2 37.0 %collective-permute-start.32 = (bf16[768,768]{1,0:T(8,128)(2,1)}, bf16[768,768]{1,0:T(8,128)(2,1)}, u32[]{:S(2)}, u32[]{:S(2)}) collective-permute-start(bf16[768,768]{1,0:T(8,128)(2,1)} %collective-permute-done.31.w_mine.refs_5_), channel_id=1, source_target_pairs={{0,1},{1,0},{2,3},{3,2},{4,5},{5,4},{6,7},{7,6},{8,9},{9,8},{10,11... | collective-permute-start | bytes 3538952 | tf_op jit(solution)/shard_map/ppermute | solution.py:779
  223.9 53.4 %collective-permute-start.7 = (bf16[768,768]{1,0:T(8,128)(2,1)S(1)}, bf16[768,768]{1,0:T(8,128)(2,1)}, u32[]{:S(2)}, u32[]{:S(2)}) collective-permute-start(bf16[768,768]{1,0:T(8,128)(2,1)S(1)} %constant_dynamic-update-slice_fusion.w_mine.refs_10_), channel_id=1, source_target_pairs={{0,1},{1,0},{2,3},{3,2},{4,5},{5,4},{6,7},{7,6},{8,9},{9,8},{10,11... | collective-permute-start | bytes 3538952 | tf_op jit(solution)/shard_map/ppermute | solution.py:779
  224.3 70.5 %collective-permute-start.35 = (bf16[768,768]{1,0:T(8,128)(2,1)S(1)}, bf16[768,768]{1,0:T(8,128)(2,1)}, u32[]{:S(2)}, u32[]{:S(2)}) collective-permute-start(bf16[768,768]{1,0:T(8,128)(2,1)S(1)} %constant_dynamic-update-slice_fusion.2.w_mine.refs_7_), channel_id=1, source_target_pairs={{0,1},{1,0},{2,3},{3,2},{4,5},{5,4},{6,7},{7,6},{8,9},{9,8},{10,11... | collective-permute-start | bytes 3538952 | tf_op jit(solution)/shard_map/ppermute | solution.py:779
  238.1 23.3 %collective-permute-start.19 = (bf16[2,128,384]{2,1,0:T(8,128)(2,1)S(1)}, bf16[2,128,384]{2,1,0:T(8,128)(2,1)S(1)}, u32[]{:S(2)}, u32[]{:S(2)}) collective-permute-start(bf16[2,128,384]{2,1,0:T(8,128)(2,1)S(1)} %constant_dynamic-slice_fusion.20), channel_id=1, source_target_pairs={{0,1},{1,0},{2,3},{3,2},{4,5},{5,4},{6,7},{7,6},{8,9},{9,8},{10,11... | collective-permute-start | bytes 589832 | tf_op jit(solution)/shard_map/ppermute | solution.py:779
  247.9 15.0 %collective-permute-start.14 = (bf16[2,128,384]{2,1,0:T(8,128)(2,1)S(1)}, bf16[2,128,384]{2,1,0:T(8,128)(2,1)S(1)}, u32[]{:S(2)}, u32[]{:S(2)}) collective-permute-start(bf16[2,128,384]{2,1,0:T(8,128)(2,1)S(1)} %constant_dynamic-slice_fusion.25), channel_id=1, source_target_pairs={{0,1},{1,0},{2,3},{3,2},{4,5},{5,4},{6,7},{7,6},{8,9},{9,8},{10,11... | collective-permute-start | bytes 589832 | tf_op jit(solution)/shard_map/ppermute | solution.py:779
  261.6 14.0 %collective-permute-start.20 = (bf16[2,128,384]{2,1,0:T(8,128)(2,1)S(1)}, bf16[2,128,384]{2,1,0:T(8,128)(2,1)S(1)}, u32[]{:S(2)}, u32[]{:S(2)}) collective-permute-start(bf16[2,128,384]{2,1,0:T(8,128)(2,1)S(1)} %get-tuple-element.191), channel_id=1, source_target_pairs={{0,2},{1,3},{8,10},{9,11},{16,18},{17,19},{24,26},{25,27}} | collective-permute-start | bytes 589832 | tf_op jit(solution)/shard_map/ppermute | solution.py:805
  263.0 13.4 %collective-permute-start.15 = (bf16[2,128,384]{2,1,0:T(8,128)(2,1)S(1)}, bf16[2,128,384]{2,1,0:T(8,128)(2,1)S(1)}, u32[]{:S(2)}, u32[]{:S(2)}) collective-permute-start(bf16[2,128,384]{2,1,0:T(8,128)(2,1)S(1)} %get-tuple-element.196), channel_id=1, source_target_pairs={{0,2},{1,3},{8,10},{9,11},{16,18},{17,19},{24,26},{25,27}} | collective-permute-start | bytes 589832 | tf_op jit(solution)/shard_map/ppermute | solution.py:805
  286.0 13.7 %collective-permute-start.22 = (bf16[2,128,384]{2,1,0:T(8,128)(2,1)S(1)}, bf16[2,128,384]{2,1,0:T(8,128)(2,1)S(1)}, u32[]{:S(2)}, u32[]{:S(2)}) collective-permute-start(bf16[2,128,384]{2,1,0:T(8,128)(2,1)S(1)} %get-tuple-element.189), channel_id=1, source_target_pairs={{4,6},{5,7},{12,14},{13,15},{20,22},{21,23},{28,30},{29,31}} | collective-permute-start | bytes 589832 | tf_op jit(solution)/shard_map/ppermute | solution.py:805
  286.8 14.1 %collective-permute-start.17 = (bf16[2,128,384]{2,1,0:T(8,128)(2,1)S(1)}, bf16[2,128,384]{2,1,0:T(8,128)(2,1)S(1)}, u32[]{:S(2)}, u32[]{:S(2)}) collective-permute-start(bf16[2,128,384]{2,1,0:T(8,128)(2,1)S(1)} %get-tuple-element.194), channel_id=1, source_target_pairs={{4,6},{5,7},{12,14},{13,15},{20,22},{21,23},{28,30},{29,31}} | collective-permute-start | bytes 589832 | tf_op jit(solution)/shard_map/ppermute | solution.py:805
  287.7 11.2 %collective-permute-start.25 = (bf16[2,128,384]{2,1,0:T(8,128)(2,1)S(1)}, bf16[2,128,384]{2,1,0:T(8,128)(2,1)S(1)}, u32[]{:S(2)}, u32[]{:S(2)}) collective-permute-start(bf16[2,128,384]{2,1,0:T(8,128)(2,1)S(1)} %get-tuple-element.186), channel_id=1, source_target_pairs={{0,2},{1,3},{8,10},{9,11},{16,18},{17,19},{24,26},{25,27}} | collective-permute-start | bytes 589832 | tf_op jit(solution)/shard_map/ppermute | solution.py:805
  345.2 38.3 %collective-permute-start.36 = (bf16[2,128,384]{2,1,0:T(8,128)(2,1)}, bf16[2,128,384]{2,1,0:T(8,128)(2,1)}, u32[]{:S(2)}, u32[]{:S(2)}) collective-permute-start(bf16[2,128,384]{2,1,0:T(8,128)(2,1)} %get-tuple-element.222), channel_id=1, source_target_pairs={{0,1},{1,0},{2,3},{3,2},{4,5},{5,4},{6,7},{7,6},{8,9},{9,8},{10,11... | collective-permute-start | bytes 589832 | tf_op jit(solution)/shard_map/ppermute | solution.py:779
  345.5 38.1 %collective-permute-start.41 = (bf16[2,128,384]{2,1,0:T(8,128)(2,1)}, bf16[2,128,384]{2,1,0:T(8,128)(2,1)}, u32[]{:S(2)}, u32[]{:S(2)}) collective-permute-start(bf16[2,128,384]{2,1,0:T(8,128)(2,1)} %get-tuple-element.221), channel_id=1, source_target_pairs={{0,1},{1,0},{2,3},{3,2},{4,5},{5,4},{6,7},{7,6},{8,9},{9,8},{10,11... | collective-permute-start | bytes 589832 | tf_op jit(solution)/shard_map/ppermute | solution.py:779
  345.8 37.8 %collective-permute-start.46 = (bf16[2,128,384]{2,1,0:T(8,128)(2,1)}, bf16[2,128,384]{2,1,0:T(8,128)(2,1)}, u32[]{:S(2)}, u32[]{:S(2)}) collective-permute-start(bf16[2,128,384]{2,1,0:T(8,128)(2,1)} %get-tuple-element.220), channel_id=1, source_target_pairs={{0,1},{1,0},{2,3},{3,2},{4,5},{5,4},{6,7},{7,6},{8,9},{9,8},{10,11... | collective-permute-start | bytes 589832 | tf_op jit(solution)/shard_map/ppermute | solution.py:779
  346.0 37.6 %collective-permute-start.51 = (bf16[2,128,384]{2,1,0:T(8,128)(2,1)}, bf16[2,128,384]{2,1,0:T(8,128)(2,1)}, u32[]{:S(2)}, u32[]{:S(2)}) collective-permute-start(bf16[2,128,384]{2,1,0:T(8,128)(2,1)} %get-tuple-element.219), channel_id=1, source_target_pairs={{0,1},{1,0},{2,3},{3,2},{4,5},{5,4},{6,7},{7,6},{8,9},{9,8},{10,11... | collective-permute-start | bytes 589832 | tf_op jit(solution)/shard_map/ppermute | solution.py:779
  349.5 192.0 %reduce-scatter.5.cloned.1.call-start = ((), (), s32[]{:S(2)}) async-start(), calls=%async_computation.8 | async-start | bytes 884736 | tf_op jit(solution)/shard_map/reduce_scatter | solution.py:984
  386.7 17.7 %collective-permute-start.42 = (bf16[2,128,384]{2,1,0:T(8,128)(2,1)}, bf16[2,128,384]{2,1,0:T(8,128)(2,1)S(1)}, u32[]{:S(2)}, u32[]{:S(2)}) collective-permute-start(bf16[2,128,384]{2,1,0:T(8,128)(2,1)} %get-tuple-element.213), channel_id=1, source_target_pairs={{6,4},{7,5},{14,12},{15,13},{22,20},{23,21},{30,28},{31,29}} | collective-permute-start | bytes 589832 | tf_op jit(solution)/shard_map/ppermute | solution.py:805
  408.1 23.9 %collective-permute-start.44 = (bf16[2,128,384]{2,1,0:T(8,128)(2,1)S(1)}, bf16[2,128,384]{2,1,0:T(8,128)(2,1)S(1)}, u32[]{:S(2)}, u32[]{:S(2)}) collective-permute-start(bf16[2,128,384]{2,1,0:T(8,128)(2,1)S(1)} %get-tuple-element.174), channel_id=1, source_target_pairs={{2,0},{3,1},{10,8},{11,9},{18,16},{19,17},{26,24},{27,25}} | collective-permute-start | bytes 589832 | tf_op jit(solution)/shard_map/ppermute | solution.py:805
  409.5 26.9 %collective-permute-start.39 = (bf16[2,128,384]{2,1,0:T(8,128)(2,1)S(1)}, bf16[2,128,384]{2,1,0:T(8,128)(2,1)S(1)}, u32[]{:S(2)}, u32[]{:S(2)}) collective-permute-start(bf16[2,128,384]{2,1,0:T(8,128)(2,1)S(1)} %get-tuple-element.179), channel_id=1, source_target_pairs={{2,0},{3,1},{10,8},{11,9},{18,16},{19,17},{26,24},{27,25}} | collective-permute-start | bytes 589832 | tf_op jit(solution)/shard_map/ppermute | solution.py:805
  411.0 28.8 %collective-permute-start.49 = (bf16[2,128,384]{2,1,0:T(8,128)(2,1)S(1)}, bf16[2,128,384]{2,1,0:T(8,128)(2,1)S(1)}, u32[]{:S(2)}, u32[]{:S(2)}) collective-permute-start(bf16[2,128,384]{2,1,0:T(8,128)(2,1)S(1)} %get-tuple-element.169), channel_id=1, source_target_pairs={{2,0},{3,1},{10,8},{11,9},{18,16},{19,17},{26,24},{27,25}} | collective-permute-start | bytes 589832 | tf_op jit(solution)/shard_map/ppermute | solution.py:805
  412.5 31.0 %collective-permute-start.54 = (bf16[2,128,384]{2,1,0:T(8,128)(2,1)S(1)}, bf16[2,128,384]{2,1,0:T(8,128)(2,1)S(1)}, u32[]{:S(2)}, u32[]{:S(2)}) collective-permute-start(bf16[2,128,384]{2,1,0:T(8,128)(2,1)S(1)} %get-tuple-element.164), channel_id=1, source_target_pairs={{2,0},{3,1},{10,8},{11,9},{18,16},{19,17},{26,24},{27,25}} | collective-permute-start | bytes 589832 | tf_op jit(solution)/shard_map/ppermute | solution.py:805
  432.1 11.6 %collective-permute-start.45 = (bf16[2,128,384]{2,1,0:T(8,128)(2,1)S(1)}, bf16[2,128,384]{2,1,0:T(8,128)(2,1)S(1)}, u32[]{:S(2)}, u32[]{:S(2)}) collective-permute-start(bf16[2,128,384]{2,1,0:T(8,128)(2,1)S(1)} %get-tuple-element.230), channel_id=1, source_target_pairs={{0,1},{1,0},{2,3},{3,2},{4,5},{5,4},{6,7},{7,6},{8,9},{9,8},{10,11... | collective-permute-start | bytes 589832 | tf_op jit(solution)/shard_map/ppermute | solution.py:779
  436.6 16.5 %collective-permute-start.40 = (bf16[2,128,384]{2,1,0:T(8,128)(2,1)S(1)}, bf16[2,128,384]{2,1,0:T(8,128)(2,1)S(1)}, u32[]{:S(2)}, u32[]{:S(2)}) collective-permute-start(bf16[2,128,384]{2,1,0:T(8,128)(2,1)S(1)} %get-tuple-element.232), channel_id=1, source_target_pairs={{0,1},{1,0},{2,3},{3,2},{4,5},{5,4},{6,7},{7,6},{8,9},{9,8},{10,11... | collective-permute-start | bytes 589832 | tf_op jit(solution)/shard_map/ppermute | solution.py:779
  439.9 22.5 %collective-permute-start.50 = (bf16[2,128,384]{2,1,0:T(8,128)(2,1)S(1)}, bf16[2,128,384]{2,1,0:T(8,128)(2,1)S(1)}, u32[]{:S(2)}, u32[]{:S(2)}) collective-permute-start(bf16[2,128,384]{2,1,0:T(8,128)(2,1)S(1)} %get-tuple-element.228), channel_id=1, source_target_pairs={{0,1},{1,0},{2,3},{3,2},{4,5},{5,4},{6,7},{7,6},{8,9},{9,8},{10,11... | collective-permute-start | bytes 589832 | tf_op jit(solution)/shard_map/ppermute | solution.py:779
  443.6 28.2 %collective-permute-start.55 = (bf16[2,128,384]{2,1,0:T(8,128)(2,1)S(1)}, bf16[2,128,384]{2,1,0:T(8,128)(2,1)S(1)}, u32[]{:S(2)}, u32[]{:S(2)}) collective-permute-start(bf16[2,128,384]{2,1,0:T(8,128)(2,1)S(1)} %get-tuple-element.226), channel_id=1, source_target_pairs={{0,1},{1,0},{2,3},{3,2},{4,5},{5,4},{6,7},{7,6},{8,9},{9,8},{10,11... | collective-permute-start | bytes 589832 | tf_op jit(solution)/shard_map/ppermute | solution.py:779
  509.2 67.0 %reduce-scatter.9.cloned.1.call-start = ((), (), s32[]{:S(2)}) async-start(), calls=%async_computation.10 | async-start | bytes 1769472 | tf_op jit(solution)/shard_map/reduce_scatter | solution.py:984
  513.4 104.5 %reduce-scatter.7.cloned.1.call-start = ((), (), s32[]{:S(2)}) async-start(), calls=%async_computation.9 | async-start | bytes 3686400 | tf_op jit(solution)/shard_map/reduce_scatter | solution.py:984
  518.1 154.2 %all-reduce.6.cloned.1.call-start = ((), (), s32[]{:S(2)}) async-start(), calls=%async_computation.12 | async-start | bytes 1835008 | tf_op jit(solution)/shard_map/psum | solution.py:984
  (189 other events, 1700.5 us)
Sparse Core Ops, SparseCore 0:
  10.2 25.6 all-gather.6
  38.2 31.0 all-gather.4
  71.0 30.8 all-gather.8
  103.3 89.7 all-gather.10
  349.7 39.8 reduce-scatter.10
  509.3 32.1 reduce-scatter.4
  543.8 32.3 reduce-scatter.8
  578.5 39.3 reduce-scatter.6
  622.3 50.0 all-reduce.5
